TPU v7x, 32 devices: a whole 2x2x4 slice. The times are simulated.
32 devices in a mesh: il: 4 (over y, x), xl: 2 (over core), ta: 4 (over z).
Axes of the slice: x: 2, y: 2, z: 4, core: 2. Of those that a mesh axis runs over, the one named last changes fastest.
Arguments:
- traces: float32 [128, 64, 512], P('il', 'xl', 'ta'), may hold values from -6 to 6
- live: int32 [128, 64], P('il', 'xl'), may hold values 0 or 1
- counts: int32 [4, 2, 8], P('il', None, 'ta'), may hold values from 2 to 4, as said below
- levels: int32 [4], replicated, may hold values from 100 to 1500, as said below
Outputs:
- reconstructed: float32 [128, 64, 512], P('il', 'xl', 'ta')
Inputs may be any that keep to these rules, and one draw needn't show every extreme that they name: counts[i, x, 2 t + w] is the iteration count of window w of the block of tile (i, x, t); a value of 4 occurs in every draw. `levels`: non-increasing over the iterations.
All inputs are finite; a program needn't handle non-finite values. No bound on the sum of `live` on one device may be relied on, other than what follows from the above.
Results may differ from a plain program's by a relative error of at most 0.0003.
Values may be sent and summed in bfloat16 or wider, within the bound.
A program may use at most 64 MiB of HBM per device.

v0:
```python
import jax
import jax.numpy as jnp
from jax import lax
from jax.sharding import PartitionSpec as P

WIN = 64
WIN_T = 128
WPD = 2
HALO = 16
HALO_T = 32
CORE_T = 64


highest = lax.Precision.HIGHEST


def padded(block, sides, width):
    for axis, dim in sides:
        count = lax.axis_size(axis)
        forward = [(i, i + 1) for i in range(count - 1)]
        backward = [(target, source) for source, target in forward]
        low = lax.ppermute(
            lax.slice_in_dim(block, block.shape[dim] - width, None, axis=dim), axis, forward
        )
        high = lax.ppermute(lax.slice_in_dim(block, 0, width, axis=dim), axis, backward)
        block = jnp.concatenate([low, block, high], axis=dim)
    return block


def from_partner(value, axis, stride):
    return lax.ppermute(value, axis, [(i, i ^ 1 << stride) for i in range(lax.axis_size(axis))])


def cosine_table(order):
    rows = jnp.arange(order, dtype=jnp.float32)[:, None]
    columns = jnp.arange(order, dtype=jnp.float32)[None, :]
    table = jnp.sqrt(2.0 / order) * jnp.cos(jnp.pi * (2.0 * columns + 1.0) * rows / (2.0 * order))
    scaling = jnp.where(rows == 0, jnp.sqrt(0.5), 1.0)
    return table * scaling


def taper_table(order):
    centres = jnp.arange(order, dtype=jnp.float32) + 0.5
    return jnp.sin(jnp.pi * centres / order) ** 2


def forward(volume, space_table, time_table):
    result = jnp.einsum("ak,ijk->ija", time_table, volume, precision=highest)
    result = jnp.einsum("bj,ija->iba", space_table, result, precision=highest)
    return jnp.einsum("ci,iba->cba", space_table, result, precision=highest)


def inverse(volume, space_table, time_table):
    result = jnp.einsum("ci,cba->iba", space_table, volume, precision=highest)
    result = jnp.einsum("bj,iba->ija", space_table, result, precision=highest)
    return jnp.einsum("ak,ija->ijk", time_table, result, precision=highest)


def reconstruct(window, window_mask, iterations, thresholds, space_table, time_table, taper):
    keep_part = (1.0 - window_mask)[:, :, None]

    def iterate(step_index, estimate):
        coefficients = forward(estimate, space_table, time_table)
        threshold = thresholds[step_index]
        shrunk = coefficients - jnp.clip(coefficients, -threshold, threshold)
        return window + keep_part * inverse(shrunk, space_table, time_table)

    estimate = lax.fori_loop(0, iterations, iterate, window)
    return estimate * taper


def fold_margins(block, dim, width):
    extent = block.shape[dim]
    inner = extent - 4 * width
    middle = lax.slice_in_dim(block, 2 * width, 2 * width + inner, axis=dim)
    lower_rim = lax.slice_in_dim(block, 0, width, axis=dim)
    upper_rim = lax.slice_in_dim(block, extent - width, extent, axis=dim)
    lower_pad = [(0, inner - width) if axis_number == dim else (0, 0) for axis_number in range(3)]
    upper_pad = [(inner - width, 0) if axis_number == dim else (0, 0) for axis_number in range(3)]
    return middle + jnp.pad(lower_rim, lower_pad) + jnp.pad(upper_rim, upper_pad)


def shards(traces, live, counts, levels):
    live_mask = live.astype(jnp.float32)
    timed = padded(traces * live_mask[:, :, None], (("ta", 2),), HALO_T)
    observed = padded(timed, (("il", 0), ("xl", 1)), HALO)
    live_pad = padded(live.astype(jnp.bfloat16), (("il", 0), ("xl", 1)), HALO).astype(jnp.float32)
    thresholds = levels.astype(jnp.float32) * 0.001
    space_table = cosine_table(WIN)
    time_table = cosine_table(WIN_T)
    space_taper = taper_table(WIN)
    taper = (
        space_taper[:, None, None] * space_taper[None, :, None] * taper_table(WIN_T)[None, None, :]
    )
    position = lax.axis_index("xl")
    line_counts = counts[0]
    own_counts = lax.dynamic_index_in_dim(line_counts, position, 0, keepdims=False)
    windows = [observed[:, :, slot * CORE_T : slot * CORE_T + WIN_T] for slot in range(WPD)]
    partner_counts = lax.dynamic_index_in_dim(
        line_counts, jnp.bitwise_xor(position, 1), 0, keepdims=False
    )
    own_final = own_counts[WPD - 1]
    partner_final = partner_counts[WPD - 1]
    own_rest = jnp.sum(own_counts) - own_final
    partner_rest = jnp.sum(partner_counts) - partner_final
    before = jnp.maximum(own_rest + own_final, partner_rest + partner_final)
    after = jnp.maximum(own_rest + partner_final, partner_rest + own_final)
    trading = after < before
    results = [
        reconstruct(windows[0], live_pad, own_counts[0], thresholds, space_table, time_table, taper)
    ]
    kept_result = reconstruct(
        windows[WPD - 1],
        live_pad,
        jnp.where(trading, 0, own_final),
        thresholds,
        space_table,
        time_table,
        taper,
    )
    payload = (windows[WPD - 1], live_pad, own_final.astype(jnp.float32).reshape(1))
    arrived = from_partner((payload[0], payload[1], payload[2]), "xl", 0)
    foreign_count = jnp.where(trading, arrived[2][0].astype(jnp.int32), 0)
    helped = reconstruct(
        arrived[0], arrived[1], foreign_count, thresholds, space_table, time_table, taper
    )
    returned = from_partner(helped, "xl", 0)
    results.append(jnp.where(trading, returned, kept_result))
    accumulated = jnp.pad(results[0], ((0, 0), (0, 0), (0, (WPD - 1) * CORE_T)))
    slot = 1
    accumulated = accumulated + jnp.pad(
        results[slot], ((0, 0), (0, 0), (slot * CORE_T, (WPD - 1 - slot) * CORE_T))
    )
    spread = padded(accumulated, (("il", 0), ("xl", 1)), HALO)
    spread = fold_margins(spread, 0, HALO)
    spread = fold_margins(spread, 1, HALO)
    spread = padded(spread, (("ta", 2),), HALO_T)
    return fold_margins(spread, 2, HALO_T)


def solution(mesh):
    placed = (P("il", "xl", "ta"), P("il", "xl"), P("il", None, "ta"), P())
    return jax.shard_map(
        shards, mesh=mesh, in_specs=placed, out_specs=P("il", "xl", "ta"), check_vma=False
    )
```

profile of v0, /device:TPU:0, one launch (start us, length us, event | category | flops | bytes accessed | tf_op | source)
XLA Modules:
  0.0 300.4 jit_solution(11374999662803267775)
XLA Ops:
  4.8 4.4 %collective-permute-start.6 = (bf16[16,32]{1,0:T(8,128)(2,1)S(1)}, bf16[16,32]{1,0:T(8,128)(2,1)S(1)}, u32[]{:S(2)}, u32[]{:S(2)}) collective-permute-start(bf16[16,32]{1,0:T(8,128)(2,1)S(1)} %get-tuple-element.421), channel_id=1, source_target_pairs={{0,8},{8,16},{16,24},{1,9},{9,17},{17,25},{2,10},{10,18},{18,26},{... | collective-permute-start | bytes 3080 | tf_op jit(solution)/shard_map/ppermute | solution.py:22
  12.0 3.5 %collective-permute-start = (f32[32,32,32]{2,1,0:T(8,128)S(1)}, f32[32,32,32]{2,1,0:T(8,128)S(1)}, u32[]{:S(2)}, u32[]{:S(2)}) collective-permute-start(f32[32,32,32]{2,1,0:T(8,128)S(1)} %get-tuple-element.411), channel_id=1, source_target_pairs={{0,1},{1,2},{2,3},{4,5},{5,6},{6,7},{8,9},{9,10},{10,11},{12,13},{... | collective-permute-start | bytes 393224 | tf_op jit(solution)/shard_map/ppermute | solution.py:22
  16.9 10.1 %collective-permute-done = f32[32,32,32]{2,1,0:T(8,128)S(1)} collective-permute-done((f32[32,32,32]{2,1,0:T(8,128)S(1)}, f32[32,32,32]{2,1,0:T(8,128)S(1)}, u32[]{:S(2)}, u32[]{:S(2)}) %collective-permute-start) | collective-permute-done | bytes 131104 | tf_op jit(solution)/shard_map/ppermute | solution.py:22
  27.0 4.1 %collective-permute-done.1 = f32[32,32,32]{2,1,0:T(8,128)S(1)} collective-permute-done((f32[32,32,32]{2,1,0:T(8,128)S(1)}, f32[32,32,32]{2,1,0:T(8,128)S(1)}, u32[]{:S(2)}, u32[]{:S(2)}) %collective-permute-start.1) | collective-permute-done | bytes 131104 | tf_op jit(solution)/shard_map/ppermute | solution.py:25
  31.7 4.3 %collective-permute-start.2 = (f32[16,32,192]{2,1,0:T(8,128)S(1)}, f32[16,32,192]{2,1,0:T(8,128)S(1)}, u32[]{:S(2)}, u32[]{:S(2)}) collective-permute-start(f32[16,32,192]{2,1,0:T(8,128)S(1)} %get-tuple-element.409), channel_id=1, source_target_pairs={{0,8},{8,16},{16,24},{1,9},{9,17},{17,25},{2,10},{10,18},{18,26},{... | collective-permute-start | bytes 1179656 | tf_op jit(solution)/shard_map/ppermute | solution.py:22
  37.4 8.7 %collective-permute-done.2 = f32[16,32,192]{2,1,0:T(8,128)S(1)} collective-permute-done((f32[16,32,192]{2,1,0:T(8,128)S(1)}, f32[16,32,192]{2,1,0:T(8,128)S(1)}, u32[]{:S(2)}, u32[]{:S(2)}) %collective-permute-start.2) | collective-permute-done | bytes 393248 | tf_op jit(solution)/shard_map/ppermute | solution.py:22
  46.1 14.1 %collective-permute-done.3 = f32[16,32,192]{2,1,0:T(8,128)S(1)} collective-permute-done((f32[16,32,192]{2,1,0:T(8,128)S(1)}, f32[16,32,192]{2,1,0:T(8,128)S(1)}, u32[]{:S(2)}, u32[]{:S(2)}) %collective-permute-start.3) | collective-permute-done | bytes 393248 | tf_op jit(solution)/shard_map/ppermute | solution.py:25
  65.9 4.0 %collective-permute-start.8 = (bf16[64,16]{1,0:T(8,128)(2,1)S(1)}, bf16[64,16]{1,0:T(8,128)(2,1)S(1)}, u32[]{:S(2)}, u32[]{:S(2)}) collective-permute-start(bf16[64,16]{1,0:T(8,128)(2,1)S(1)} %get-tuple-element.415), channel_id=1, source_target_pairs={{0,4},{1,5},{2,6},{3,7},{8,12},{9,13},{10,14},{11,15},{16,20},{17,... | collective-permute-start | bytes 6152 | tf_op jit(solution)/shard_map/ppermute | solution.py:22
  80.3 3.8 %pad_maximum_fusion.1 = f32[64,64,192]{2,1,0:T(8,128)S(1)} fusion(f32[64,16,192]{2,1,0:T(8,128)} %collective-permute-done.5, f32[16,32,192]{2,1,0:T(8,128)S(1)} %collective-permute-done.3, f32[32,32,32]{2,1,0:T(8,128)S(1)} %collective-permute-done.1, f32[32,32,128]{2,1,0:T(8,128)S(1)} %broadcast_multiply_fusion, f32[32,32,32]{2,1,0:T(8,128)S(1)} %collective-permute-done, ...), kind=kLoop, calls=%fused_computation.156 | loop fusion | flops 4718592 | bytes 6291456 | tf_op jit(solution)/shard_map/concatenate | solution.py:26
  87.9 74.4 %while.36 = (s32[]{:T(128)}, f32[64,64,128]{2,1,0:T(8,128)S(1)}, s32[]{:T(128)}, f32[64,64,1]{1,0,2:T(8,128)S(1)}, f32[4]{0:T(128)S(1)}, /*index=5*/f32[64,64,12...) while((s32[]{:T(128)}, f32[64,64,128]{2,1,0:T(8,128)S(1)}, ...), condition=%wide.region_1.2_spmd.clone.clone, body=%wide.region_0.1_spmd.clone.clone.sunk | while | flops 3223994368 | bytes 35672284 | solution.py:68
  94.3 3.5 %fusion.234 = f32[64,128,64]{1,2,0:T(8,128)S(1)} fusion(f32[64,64,128]{2,1,0:T(8,128)S(1)} %convolution_bitcast_fusion.6, f32[64]{0:T(128)S(1)} %get-tuple-element.730, f32[64]{0:T(128)S(1)} %get-tuple-element.729), kind=kOutput, calls=%fused_computation.14.clone.1 | convolution fusion | flops 402665472 | bytes 4194816 | tf_op jit(solution)/shard_map/while/body/ci,iba->cba/dot_general | solution.py:50
  112.6 3.5 %fusion.234 = f32[64,128,64]{1,2,0:T(8,128)S(1)} fusion(f32[64,64,128]{2,1,0:T(8,128)S(1)} %convolution_bitcast_fusion.6, f32[64]{0:T(128)S(1)} %get-tuple-element.730, f32[64]{0:T(128)S(1)} %get-tuple-element.729), kind=kOutput, calls=%fused_computation.14.clone.1 | convolution fusion | flops 402665472 | bytes 4194816 | tf_op jit(solution)/shard_map/while/body/ci,iba->cba/dot_general | solution.py:50
  162.3 4.0 %copy.60 = f32[64,64,128]{2,1,0:T(8,128)} copy(f32[64,64,128]{2,1,0:T(8,128)} %get-tuple-element.661) | data formatting | bytes 4194304
  167.9 38.4 %while.37 = (s32[]{:T(128)}, f32[64,64,128]{2,1,0:T(8,128)S(1)}, s32[]{:T(128)}, f32[64,64,1]{1,0,2:T(8,128)S(1)}, f32[4]{0:T(128)S(1)}, /*index=5*/f32[64,64,12...) while((s32[]{:T(128)}, f32[64,64,128]{2,1,0:T(8,128)S(1)}, ...), condition=%wide.region_5.6_spmd.clone.clone, body=%wide.region_4.5_spmd.clone.clone.sunk | while | flops 3223994368 | bytes 27283652 | solution.py:68
  183.4 3.6 %multiply_add_fusion.7 = f32[64,64,128]{2,1,0:T(8,128)S(1)} fusion(f32[64,64,128]{2,1,0:T(8,128)} %get-tuple-element.648, f32[64,128,64]{1,2,0:T(8,128)S(1)} %fusion.251, f32[64,64]{1,0:T(8,128)S(1)} %bitcast.214, f32[128]{0:T(128)S(1)} %get-tuple-element.650, f32[128]{0:T(128)S(1)} %get-tuple-element.649), kind=kOutput, calls=%fused_computation.64.clone.1 | convolution fusion | flops 806404096 | bytes 6308864 | tf_op jit(solution)/shard_map/while/body/ak,ija->ijk/dot_general | solution.py:56
  192.5 3.5 %fusion.249 = f32[64,128,64]{1,2,0:T(8,128)S(1)} fusion(f32[64,64,128]{2,1,0:T(8,128)S(1)} %convolution_bitcast_fusion.7, f32[64]{0:T(128)S(1)} %get-tuple-element.652, f32[64]{0:T(128)S(1)} %get-tuple-element.651), kind=kOutput, calls=%fused_computation.62.clone.1 | convolution fusion | flops 402665472 | bytes 4194816 | tf_op jit(solution)/shard_map/while/body/ci,iba->cba/dot_general | solution.py:50
  202.5 3.6 %multiply_add_fusion.7 = f32[64,64,128]{2,1,0:T(8,128)S(1)} fusion(f32[64,64,128]{2,1,0:T(8,128)} %get-tuple-element.648, f32[64,128,64]{1,2,0:T(8,128)S(1)} %fusion.251, f32[64,64]{1,0:T(8,128)S(1)} %bitcast.214, f32[128]{0:T(128)S(1)} %get-tuple-element.650, f32[128]{0:T(128)S(1)} %get-tuple-element.649), kind=kOutput, calls=%fused_computation.64.clone.1 | convolution fusion | flops 806404096 | bytes 6308864 | tf_op jit(solution)/shard_map/while/body/ak,ija->ijk/dot_general | solution.py:56
  208.1 3.6 %while.38 = (s32[]{:T(128)}, f32[64,64,128]{2,1,0:T(8,128)}, s32[]{:T(128)}, f32[64,64,1]{1,0,2:T(8,128)S(1)}, f32[4]{0:T(128)S(1)}, /*index=5*/f32[64,64,128]{2...) while((s32[]{:T(128)}, f32[64,64,128]{2,1,0:T(8,128)}, ...), condition=%wide.region_7.8_spmd.clone.clone, body=%wide.region_6.7_spmd.clone.clone.sunk | while | flops 3223994368 | bytes 27283652 | solution.py:68
  219.6 20.5 %collective-permute-done.14 = f32[16,64,192]{2,1,0:T(8,128)S(1)} collective-permute-done((f32[16,64,192]{2,1,0:T(8,128)S(1)}, f32[16,64,192]{2,1,0:T(8,128)S(1)}, u32[]{:S(2)}, u32[]{:S(2)}) %collective-permute-start.14) | collective-permute-done | bytes 786464 | tf_op jit(solution)/shard_map/ppermute | solution.py:22
  240.1 4.2 %collective-permute-done.15 = f32[16,64,192]{2,1,0:T(8,128)S(1)} collective-permute-done((f32[16,64,192]{2,1,0:T(8,128)S(1)}, f32[16,64,192]{2,1,0:T(8,128)S(1)}, u32[]{:S(2)}, u32[]{:S(2)}) %collective-permute-start.15) | collective-permute-done | bytes 786464 | tf_op jit(solution)/shard_map/ppermute | solution.py:25
  251.4 3.7 %pad_maximum_fusion = f32[96,96,192]{2,1,0:T(8,128)S(1)} fusion(f32[96,16,192]{2,1,0:T(8,128)S(1)} %collective-permute-done.17, f32[16,64,192]{2,1,0:T(8,128)S(1)} %collective-permute-done.15, f32[64,64,192]{2,1,0:T(8,128)S(1)} %pad_add_fusion, f32[16,64,192]{2,1,0:T(8,128)S(1)} %collective-permute-done.14, f32[96,16,192]{2,1,0:T(8,128)S(1)} %collective-permute-done.16), kind=kLoop, calls=%fused_computation.150 | loop fusion | flops 7077888 | bytes 14155776 | tf_op jit(solution)/shard_map/concatenate | solution.py:26
  258.3 3.5 %collective-permute-start.18 = (f32[32,32,32]{2,1,0:T(8,128)S(1)}, f32[32,32,32]{2,1,0:T(8,128)S(1)}, u32[]{:S(2)}, u32[]{:S(2)}) collective-permute-start(f32[32,32,32]{2,1,0:T(8,128)S(1)} %get-tuple-element.407), channel_id=1, source_target_pairs={{0,1},{1,2},{2,3},{4,5},{5,6},{6,7},{8,9},{9,10},{10,11},{12,13},{... | collective-permute-start | bytes 393224 | tf_op jit(solution)/shard_map/ppermute | solution.py:22
  263.0 10.1 %collective-permute-done.18 = f32[32,32,32]{2,1,0:T(8,128)S(1)} collective-permute-done((f32[32,32,32]{2,1,0:T(8,128)S(1)}, f32[32,32,32]{2,1,0:T(8,128)S(1)}, u32[]{:S(2)}, u32[]{:S(2)}) %collective-permute-start.18) | collective-permute-done | bytes 131104 | tf_op jit(solution)/shard_map/ppermute | solution.py:22
  273.2 25.9 %collective-permute-done.19 = f32[32,32,32]{2,1,0:T(8,128)S(1)} collective-permute-done((f32[32,32,32]{2,1,0:T(8,128)S(1)}, f32[32,32,32]{2,1,0:T(8,128)S(1)}, u32[]{:S(2)}, u32[]{:S(2)}) %collective-permute-start.19) | collective-permute-done | bytes 131104 | tf_op jit(solution)/shard_map/ppermute | solution.py:25
  (117 shorter events, 134.9 us)
Async XLA Ops:
  2.7 74.8 %collective-permute-start.11 = (f32[1]{0:T(128)}, f32[1]{0:T(128)}, u32[]{:S(2)}, u32[]{:S(2)}) collective-permute-start(f32[1]{0:T(128)} %bitcast.6), channel_id=1, source_target_pairs={{0,4},{4,0},{1,5},{5,1},{2,6},{6,2},{3,7},{7,3},{8,12},{12,8},{9,1... | collective-permute-start | bytes 20 | tf_op jit(solution)/shard_map/ppermute | solution.py:31
  4.8 32.5 %collective-permute-start.6 = (bf16[16,32]{1,0:T(8,128)(2,1)S(1)}, bf16[16,32]{1,0:T(8,128)(2,1)S(1)}, u32[]{:S(2)}, u32[]{:S(2)}) collective-permute-start(bf16[16,32]{1,0:T(8,128)(2,1)S(1)} %get-tuple-element.421), channel_id=1, source_target_pairs={{0,8},{8,16},{16,24},{1,9},{9,17},{17,25},{2,10},{10,18},{18,26},{... | collective-permute-start | bytes 3080 | tf_op jit(solution)/shard_map/ppermute | solution.py:22
  9.2 28.2 %collective-permute-start.7 = (bf16[16,32]{1,0:T(8,128)(2,1)S(1)}, bf16[16,32]{1,0:T(8,128)(2,1)S(1)}, u32[]{:S(2)}, u32[]{:S(2)}) collective-permute-start(bf16[16,32]{1,0:T(8,128)(2,1)S(1)} %get-tuple-element.422), channel_id=1, source_target_pairs={{8,0},{16,8},{24,16},{9,1},{17,9},{25,17},{10,2},{18,10},{26,18},{... | collective-permute-start | bytes 3080 | tf_op jit(solution)/shard_map/ppermute | solution.py:25
  12.0 15.0 %collective-permute-start = (f32[32,32,32]{2,1,0:T(8,128)S(1)}, f32[32,32,32]{2,1,0:T(8,128)S(1)}, u32[]{:S(2)}, u32[]{:S(2)}) collective-permute-start(f32[32,32,32]{2,1,0:T(8,128)S(1)} %get-tuple-element.411), channel_id=1, source_target_pairs={{0,1},{1,2},{2,3},{4,5},{5,6},{6,7},{8,9},{9,10},{10,11},{12,13},{... | collective-permute-start | bytes 393224 | tf_op jit(solution)/shard_map/ppermute | solution.py:22
  15.5 15.7 %collective-permute-start.1 = (f32[32,32,32]{2,1,0:T(8,128)S(1)}, f32[32,32,32]{2,1,0:T(8,128)S(1)}, u32[]{:S(2)}, u32[]{:S(2)}) collective-permute-start(f32[32,32,32]{2,1,0:T(8,128)S(1)} %get-tuple-element.412), channel_id=1, source_target_pairs={{1,0},{2,1},{3,2},{5,4},{6,5},{7,6},{9,8},{10,9},{11,10},{13,12},{... | collective-permute-start | bytes 393224 | tf_op jit(solution)/shard_map/ppermute | solution.py:25
  16.9 20.4 %copy-start.5 = (s32[4]{0:T(128)S(1)}, s32[4]{0:T(128)}, u32[]{:S(2)}) copy-start(s32[4]{0:T(128)} %param.13) | copy-start | bytes 52
  31.7 14.4 %collective-permute-start.2 = (f32[16,32,192]{2,1,0:T(8,128)S(1)}, f32[16,32,192]{2,1,0:T(8,128)S(1)}, u32[]{:S(2)}, u32[]{:S(2)}) collective-permute-start(f32[16,32,192]{2,1,0:T(8,128)S(1)} %get-tuple-element.409), channel_id=1, source_target_pairs={{0,8},{8,16},{16,24},{1,9},{9,17},{17,25},{2,10},{10,18},{18,26},{... | collective-permute-start | bytes 1179656 | tf_op jit(solution)/shard_map/ppermute | solution.py:22
  36.0 24.1 %collective-permute-start.3 = (f32[16,32,192]{2,1,0:T(8,128)S(1)}, f32[16,32,192]{2,1,0:T(8,128)S(1)}, u32[]{:S(2)}, u32[]{:S(2)}) collective-permute-start(f32[16,32,192]{2,1,0:T(8,128)S(1)} %get-tuple-element.410), channel_id=1, source_target_pairs={{8,0},{16,8},{24,16},{9,1},{17,9},{25,17},{10,2},{18,10},{26,18},{... | collective-permute-start | bytes 1179656 | tf_op jit(solution)/shard_map/ppermute | solution.py:25
  62.2 18.1 %collective-permute-start.4 = (f32[64,16,192]{2,1,0:T(8,128)}, f32[64,16,192]{2,1,0:T(8,128)}, u32[]{:S(2)}, u32[]{:S(2)}) collective-permute-start(f32[64,16,192]{2,1,0:T(8,128)} %get-tuple-element.405), channel_id=1, source_target_pairs={{0,4},{1,5},{2,6},{3,7},{8,12},{9,13},{10,14},{11,15},{16,20},{17,... | collective-permute-start | bytes 2359304 | tf_op jit(solution)/shard_map/ppermute | solution.py:22
  64.5 15.8 %collective-permute-start.5 = (f32[64,16,192]{2,1,0:T(8,128)}, f32[64,16,192]{2,1,0:T(8,128)}, u32[]{:S(2)}, u32[]{:S(2)}) collective-permute-start(f32[64,16,192]{2,1,0:T(8,128)} %get-tuple-element.406), channel_id=1, source_target_pairs={{4,0},{5,1},{6,2},{7,3},{12,8},{13,9},{14,10},{15,11},{20,16},{21,... | collective-permute-start | bytes 2359304 | tf_op jit(solution)/shard_map/ppermute | solution.py:25
  65.9 12.3 %collective-permute-start.8 = (bf16[64,16]{1,0:T(8,128)(2,1)S(1)}, bf16[64,16]{1,0:T(8,128)(2,1)S(1)}, u32[]{:S(2)}, u32[]{:S(2)}) collective-permute-start(bf16[64,16]{1,0:T(8,128)(2,1)S(1)} %get-tuple-element.415), channel_id=1, source_target_pairs={{0,4},{1,5},{2,6},{3,7},{8,12},{9,13},{10,14},{11,15},{16,20},{17,... | collective-permute-start | bytes 6152 | tf_op jit(solution)/shard_map/ppermute | solution.py:22
  69.9 8.3 %collective-permute-start.9 = (bf16[64,16]{1,0:T(8,128)(2,1)S(1)}, bf16[64,16]{1,0:T(8,128)(2,1)S(1)}, u32[]{:S(2)}, u32[]{:S(2)}) collective-permute-start(bf16[64,16]{1,0:T(8,128)(2,1)S(1)} %get-tuple-element.416), channel_id=1, source_target_pairs={{4,0},{5,1},{6,2},{7,3},{12,8},{13,9},{14,10},{15,11},{20,16},{21,... | collective-permute-start | bytes 6152 | tf_op jit(solution)/shard_map/ppermute | solution.py:25
  78.3 2.0 collective-permute-start.12
  87.6 78.7 %collective-permute-start.10 = (f32[64,64,128]{2,1,0:T(8,128)}, f32[64,64,128]{2,1,0:T(8,128)}, u32[]{:S(2)}, u32[]{:S(2)}) collective-permute-start(f32[64,64,128]{2,1,0:T(8,128)} %get-tuple-element.661), channel_id=1, source_target_pairs={{0,4},{4,0},{1,5},{5,1},{2,6},{6,2},{3,7},{7,3},{8,12},{12,8},{9,1... | collective-permute-start | bytes 6291464 | tf_op jit(solution)/shard_map/ppermute | solution.py:31
  162.3 4.0 %copy-start = (f32[64,64,128]{2,1,0:T(8,128)}, f32[64,64,128]{2,1,0:T(8,128)S(1)}, u32[]{:S(2)}) copy-start(f32[64,64,128]{2,1,0:T(8,128)S(1)} %get-tuple-element.170) | copy-start | bytes 6291460
  208.1 4.5 %collective-permute-start.13 = (f32[64,64,128]{2,1,0:T(8,128)}, f32[64,64,128]{2,1,0:T(8,128)}, u32[]{:S(2)}, u32[]{:S(2)}) collective-permute-start(f32[64,64,128]{2,1,0:T(8,128)} %multiply_multiply_fusion.1), channel_id=1, source_target_pairs={{0,4},{4,0},{1,5},{5,1},{2,6},{6,2},{3,7},{7,3},{8,12},{12,8},{9,1... | collective-permute-start | bytes 6291464 | tf_op jit(solution)/shard_map/ppermute | solution.py:31
  208.1 4.5 %copy-start.1 = (f32[64,64,128]{2,1,0:T(8,128)S(1)}, f32[64,64,128]{2,1,0:T(8,128)}, u32[]{:S(2)}) copy-start(f32[64,64,128]{2,1,0:T(8,128)} %copy-done) | copy-start | bytes 6291460
  215.8 24.3 %collective-permute-start.14 = (f32[16,64,192]{2,1,0:T(8,128)S(1)}, f32[16,64,192]{2,1,0:T(8,128)S(1)}, u32[]{:S(2)}, u32[]{:S(2)}) collective-permute-start(f32[16,64,192]{2,1,0:T(8,128)S(1)} %get-tuple-element.401), channel_id=1, source_target_pairs={{0,8},{8,16},{16,24},{1,9},{9,17},{17,25},{2,10},{10,18},{18,26},{... | collective-permute-start | bytes 2359304 | tf_op jit(solution)/shard_map/ppermute | solution.py:22
  217.2 27.1 %collective-permute-start.15 = (f32[16,64,192]{2,1,0:T(8,128)S(1)}, f32[16,64,192]{2,1,0:T(8,128)S(1)}, u32[]{:S(2)}, u32[]{:S(2)}) collective-permute-start(f32[16,64,192]{2,1,0:T(8,128)S(1)} %get-tuple-element.402), channel_id=1, source_target_pairs={{8,0},{16,8},{24,16},{9,1},{17,9},{25,17},{10,2},{18,10},{26,18},{... | collective-permute-start | bytes 2359304 | tf_op jit(solution)/shard_map/ppermute | solution.py:25
  244.7 4.3 %collective-permute-start.16 = (f32[96,16,192]{2,1,0:T(8,128)S(1)}, f32[96,16,192]{2,1,0:T(8,128)S(1)}, u32[]{:S(2)}, u32[]{:S(2)}) collective-permute-start(f32[96,16,192]{2,1,0:T(8,128)S(1)} %get-tuple-element.399), channel_id=1, source_target_pairs={{0,4},{1,5},{2,6},{3,7},{8,12},{9,13},{10,14},{11,15},{16,20},{17,... | collective-permute-start | bytes 3538952 | tf_op jit(solution)/shard_map/ppermute | solution.py:22
  246.1 9.0 %copy-start.4 = (pred[32]{0:T(512)(128)(4,1)S(1)}, pred[32]{0:T(512)(128)(4,1)}, u32[]{:S(2)}) copy-start(pred[32]{0:T(512)(128)(4,1)} %constant.82.clone.1) | copy-start | bytes 100
  246.1 5.3 %collective-permute-start.17 = (f32[96,16,192]{2,1,0:T(8,128)S(1)}, f32[96,16,192]{2,1,0:T(8,128)S(1)}, u32[]{:S(2)}, u32[]{:S(2)}) collective-permute-start(f32[96,16,192]{2,1,0:T(8,128)S(1)} %get-tuple-element.400), channel_id=1, source_target_pairs={{4,0},{5,1},{6,2},{7,3},{12,8},{13,9},{14,10},{15,11},{20,16},{21,... | collective-permute-start | bytes 3538952 | tf_op jit(solution)/shard_map/ppermute | solution.py:25
  258.3 14.9 %collective-permute-start.18 = (f32[32,32,32]{2,1,0:T(8,128)S(1)}, f32[32,32,32]{2,1,0:T(8,128)S(1)}, u32[]{:S(2)}, u32[]{:S(2)}) collective-permute-start(f32[32,32,32]{2,1,0:T(8,128)S(1)} %get-tuple-element.407), channel_id=1, source_target_pairs={{0,1},{1,2},{2,3},{4,5},{5,6},{6,7},{8,9},{9,10},{10,11},{12,13},{... | collective-permute-start | bytes 393224 | tf_op jit(solution)/shard_map/ppermute | solution.py:22
  261.7 37.3 %collective-permute-start.19 = (f32[32,32,32]{2,1,0:T(8,128)S(1)}, f32[32,32,32]{2,1,0:T(8,128)S(1)}, u32[]{:S(2)}, u32[]{:S(2)}) collective-permute-start(f32[32,32,32]{2,1,0:T(8,128)S(1)} %get-tuple-element.408), channel_id=1, source_target_pairs={{1,0},{2,1},{3,2},{5,4},{6,5},{7,6},{9,8},{10,9},{11,10},{13,12},{... | collective-permute-start | bytes 393224 | tf_op jit(solution)/shard_map/ppermute | solution.py:25
  (5 other events, 15.1 us)
where the time goes:
time: 305 us; the launch traced here: 300 us
  waiting for transfers between devices  103 us (34%)
  matrix products  101 us (33%)
  starting transfers between devices  37.8 us (12%)
  other arithmetic  22.9 us (8%)
  local copies, waits for them, and re-layouts  16.3 us (5%)
  loops' own time  11.7 us (4%)
  between operations  7.51 us (2%)
    ppermute x8, waiting for transfers between devices, padded(): lax.ppermute(lax.slice_in_dim(block, block.shape[dim] - width, None, axis...  51 us
    ppermute x8, waiting for transfers between devices, padded(): lax.ppermute(lax.slice_in_dim(block, 0, width, axis=dim), axis, backward)  50.7 us
    ppermute x8, starting transfers between devices, padded(): lax.ppermute(lax.slice_in_dim(block, block.shape[dim] - width, None, axis...  24.7 us
    dot_general x6, matrix products, forward(): return jnp.einsum('ci,iba->cba', space_table, result, precision=highest)  20.7 us
    dot_general x6, matrix products, inverse(): result = jnp.einsum('bj,iba->ija', space_table, result, precision=highest)  20.6 us
    dot_general x6, matrix products, inverse(): result = jnp.einsum('ci,cba->iba', space_table, volume, precision=highest)  18.3 us
    dot_general x6, matrix products, inverse(): return jnp.einsum('ak,ija->ijk', time_table, result, precision=highest)  15.7 us
    dot_general x6, matrix products, forward(): result = jnp.einsum('bj,ija->iba', space_table, result, precision=highest)  13.1 us
  transfers between devices with their start and end apart: 20, of which 12 were waited for; matrix products, arithmetic and copies ran while one was open for 26% of the time, Pallas kernels for 0%

commit v1 on v0

v1 whole, which is shorter than its diff:
```python
import functools

import jax
import jax.numpy as jnp
import numpy as np
from jax import lax
from jax.experimental import pallas as pl
from jax.experimental.pallas import tpu as pltpu
from jax.sharding import PartitionSpec as P

WIN = 64
WIN_T = 128
WPD = 2
HALO = 16
HALO_T = 32
CORE_T = 64
DEAD = 1e30
PITCH = 72
GROUP = 16


def padded(block, sides, width):
    for axis, dim in sides:
        count = lax.axis_size(axis)
        forward = [(i, i + 1) for i in range(count - 1)]
        backward = [(target, source) for source, target in forward]
        low = lax.ppermute(
            lax.slice_in_dim(block, block.shape[dim] - width, None, axis=dim), axis, forward
        )
        high = lax.ppermute(lax.slice_in_dim(block, 0, width, axis=dim), axis, backward)
        block = jnp.concatenate([low, block, high], axis=dim)
    return block


def from_partner(value, axis, stride):
    return lax.ppermute(value, axis, [(i, i ^ 1 << stride) for i in range(lax.axis_size(axis))])


def cosine_table(order):
    rows = np.arange(order, dtype=np.float64)[:, None]
    columns = np.arange(order, dtype=np.float64)[None, :]
    table = np.sqrt(2.0 / order) * np.cos(np.pi * (2.0 * columns + 1.0) * rows / (2.0 * order))
    return table * np.where(rows == 0, np.sqrt(0.5), 1.0)


def taper_table(order):
    centres = np.arange(order, dtype=np.float64) + 0.5
    return np.sin(np.pi * centres / order) ** 2


def halves(table):
    high = table.astype(jnp.bfloat16)
    low = (table - high.astype(np.float64)).astype(jnp.bfloat16)
    return high, low


def tables():
    out = []
    space = cosine_table(WIN)
    for table in (space, space.T):
        high, low = halves(table)
        out.append(np.concatenate([high, high, low], axis=1))
    time = cosine_table(WIN_T)
    for table in (time.T, time):
        high, low = halves(table)
        row = np.concatenate([high, low], axis=1)
        out.append(np.concatenate([row, row], axis=0))
    plane = taper_table(WIN)[:, None] * taper_table(WIN_T)[None, :]
    lines = np.repeat(taper_table(WIN)[:, None], WIN_T, axis=1)
    return [jnp.asarray(t) for t in out] + [
        jnp.asarray(plane, jnp.float32),
        jnp.asarray(lines, jnp.float32),
    ]


def split(value):
    high = value.astype(jnp.bfloat16)
    low = (value - high.astype(jnp.float32)).astype(jnp.bfloat16)
    return high, low


def along_rows(table, slices):
    out = []
    for n in range(0, len(slices), 2):
        high, low = split(jnp.concatenate([slices[n], slices[n + 1]], axis=1))
        both = jnp.dot(
            table, jnp.concatenate([high, low, high], axis=0), preferred_element_type=jnp.float32
        )
        out += [both[:, :WIN_T], both[:, WIN_T:]]
    return out


def along_lanes(table, slices):
    high, low = split(jnp.concatenate(slices, axis=0))
    both = jnp.dot(
        jnp.concatenate([high, low], axis=1), table, preferred_element_type=jnp.float32
    )
    total = both[:, :WIN_T] + both[:, WIN_T:]
    return [total[n * WIN : (n + 1) * WIN] for n in range(len(slices))]


def shrink_kernel(
    counts, levels, window, space_f, space_b, time_f, time_b, plane, lines, out, held
):
    slot = pl.program_id(0)
    last = counts[slot] - 1

    def forward(group, estimates):
        done = along_rows(space_f[...], along_lanes(time_f[...], estimates))
        for n in range(GROUP):
            start = pl.multiple_of((group * GROUP + n) * PITCH, 8)
            held[pl.ds(start, WIN), :] = done[n]

    def recorded(group, n):
        start = pl.multiple_of((group * GROUP + n) * WIN, 8)
        return window[0, pl.ds(start, WIN), :]

    def backward(group):
        slices = []
        for n in range(GROUP):
            start = pl.multiple_of((group * GROUP + n) * PITCH, 8)
            slices.append(held[pl.ds(start, WIN), :])
        guesses = along_lanes(time_b[...], along_rows(space_b[...], slices))
        estimates = []
        for n in range(GROUP):
            known = recorded(group, n)
            estimates.append(jnp.where(known == DEAD, guesses[n], known))
        return estimates

    @pl.loop(0, WIN // GROUP)
    def _(group):
        estimates = []
        for n in range(GROUP):
            known = recorded(group, n)
            estimates.append(jnp.where(known == DEAD, 0.0, known))
        forward(group, estimates)

    def shrink(step):
        threshold = levels[step].astype(jnp.float32) * 0.001

        @pl.loop(0, WIN // GROUP)
        def _(group):
            first = group * GROUP
            places = [pl.ds(first + n, WIN, stride=PITCH) for n in range(GROUP)]
            values = along_rows(space_f[...], [held[p, :] for p in places])
            values = [v - jnp.clip(v, -threshold, threshold) for v in values]
            values = along_rows(space_b[...], values)
            for n in range(GROUP):
                held[places[n], :] = values[n]

    @pl.loop(0, last)
    def _(step):
        shrink(step)

        @pl.loop(0, WIN // GROUP)
        def _(group):
            forward(group, backward(group))

    shrink(last)

    @pl.loop(0, WIN // GROUP)
    def _(group):
        estimates = backward(group)
        for n in range(GROUP):
            line = group * GROUP + n
            start = pl.multiple_of(line * WIN, 8)
            weight = lines[pl.ds(line, 1), :]
            out[0, pl.ds(start, WIN), :] = estimates[n] * (plane[...] * weight)


def reconstruct(windows, counts, levels):
    slots = windows.shape[0]
    fixed = tables()
    whole = [pl.BlockSpec(memory_space=pltpu.VMEM)] * len(fixed)
    block = pl.BlockSpec((1, WIN * WIN, WIN_T), lambda slot, counts, levels: (slot, 0, 0))
    return pl.pallas_call(
        shrink_kernel,
        grid_spec=pltpu.PrefetchScalarGridSpec(
            num_scalar_prefetch=2,
            grid=(slots,),
            in_specs=[block] + whole,
            out_specs=block,
            scratch_shapes=[pltpu.VMEM((WIN * PITCH, WIN_T), jnp.float32)],
        ),
        out_shape=jax.ShapeDtypeStruct(windows.shape, jnp.float32),
        compiler_params=pltpu.CompilerParams(vmem_limit_bytes=40 * 2**20),
        name="shrink",
    )(counts, levels, windows, *fixed)


def fold_margins(block, dim, width):
    extent = block.shape[dim]
    inner = extent - 4 * width
    middle = lax.slice_in_dim(block, 2 * width, 2 * width + inner, axis=dim)
    lower_rim = lax.slice_in_dim(block, 0, width, axis=dim)
    upper_rim = lax.slice_in_dim(block, extent - width, extent, axis=dim)
    lower_pad = [(0, inner - width) if axis_number == dim else (0, 0) for axis_number in range(3)]
    upper_pad = [(inner - width, 0) if axis_number == dim else (0, 0) for axis_number in range(3)]
    return middle + jnp.pad(lower_rim, lower_pad) + jnp.pad(upper_rim, upper_pad)


def shards(traces, live, counts, levels):
    live_mask = live.astype(jnp.float32)
    timed = padded(traces * live_mask[:, :, None], (("ta", 2),), HALO_T)
    observed = padded(timed, (("il", 0), ("xl", 1)), HALO)
    live_pad = padded(live.astype(jnp.bfloat16), (("il", 0), ("xl", 1)), HALO).astype(jnp.float32)
    observed = jnp.where(live_pad[:, :, None] == 0.0, DEAD, observed)
    position = lax.axis_index("xl")
    line_counts = counts[0]
    own = lax.dynamic_index_in_dim(line_counts, position, 0, keepdims=False)
    other = lax.dynamic_index_in_dim(line_counts, jnp.bitwise_xor(position, 1), 0, keepdims=False)
    before = jnp.maximum(own[0] + own[1], other[0] + other[1])
    after = jnp.maximum(own[0] + other[1], other[0] + own[1])
    trading = after < before
    windows = [
        observed[:, :, slot * CORE_T : slot * CORE_T + WIN_T].reshape(WIN * WIN, WIN_T)
        for slot in range(WPD)
    ]
    arrived = from_partner(windows[1], "xl", 0)
    windows[1] = jnp.where(trading, arrived, windows[1])
    work = jnp.stack([own[0], jnp.where(trading, other[1], own[1])])
    done = reconstruct(jnp.stack(windows), work, levels)
    results = [done[0], jnp.where(trading, from_partner(done[1], "xl", 0), done[1])]
    results = [r.reshape(WIN, WIN, WIN_T) for r in results]
    accumulated = jnp.pad(results[0], ((0, 0), (0, 0), (0, CORE_T)))
    accumulated = accumulated + jnp.pad(results[1], ((0, 0), (0, 0), (CORE_T, 0)))
    spread = padded(accumulated, (("il", 0), ("xl", 1)), HALO)
    spread = fold_margins(spread, 0, HALO)
    spread = fold_margins(spread, 1, HALO)
    spread = padded(spread, (("ta", 2),), HALO_T)
    return fold_margins(spread, 2, HALO_T)


def solution(mesh):
    placed = (P("il", "xl", "ta"), P("il", "xl"), P("il", None, "ta"), P())
    return jax.shard_map(
        shards, mesh=mesh, in_specs=placed, out_specs=P("il", "xl", "ta"), check_vma=False
    )
```

time: 305 us -> 207 us (0.68); the launches traced: 300 us -> 206 us
  matrix products: 101 us -> 0 us
  Pallas kernels: 0 us -> 33.6 us
  loops' own time: 11.7 us -> 0 us
  local copies, waits for them, and re-layouts: 16.3 us -> 4.76 us
  starting transfers between devices: 37.8 us -> 43.6 us
  waiting for transfers between devices: 103 us -> 98.1 us
  other arithmetic: 22.9 us -> 19.5 us
    dot_general x36 -> x0, matrix products: 101 us -> none  [the longest x6 20.7 us: forward(): return jnp.einsum('ci,iba->cba', space_table, result, precision=highest)]
    pallas_call x0 -> x1, Pallas kernels: none -> 33.6 us  [reconstruct(): pl.pallas_call(shrink_kernel, grid_spec=pltpu.PrefetchScalarGridSpec(num_...]
    another operation x3 -> x0, loops' own time: 11.7 us -> none  [reconstruct(): estimate = lax.fori_loop(0, iterations, iterate, window)]
    ppermute x8, starting transfers between devices: 24.7 us -> 32.5 us  [padded(): lax.ppermute(lax.slice_in_dim(block, block.shape[dim] - width, None, axis...]
    ppermute x8, waiting for transfers between devices: 50.7 us -> 43.6 us  [padded(): lax.ppermute(lax.slice_in_dim(block, 0, width, axis=dim), axis, backward)]
    unnamed x13 -> x20, local copies, waits for them, and re-layouts: 6.91 us -> 0.95 us
    dynamic_slice x6 -> x1, local copies, waits for them, and re-layouts: 3.8 us -> 0.01 us  [shards(): lax.dynamic_index_in_dim(line_counts, jnp.bitwise_xor(position, 1), 0, ke...]
    concatenate x5 -> x4, other arithmetic: 8.41 us -> 4.66 us  [padded(): block = jnp.concatenate([low, block, high], axis=dim)]
  transfers between devices with their start and end apart: 20 -> 18, of which waited for: 12 -> 13; matrix products, arithmetic and copies ran while one was open for 26% -> 1% of each run, Pallas kernels for 0% -> 0%
where the time goes in v1:
time: 207 us; the launch traced here: 206 us
  waiting for transfers between devices  98.1 us (47%)
  starting transfers between devices  43.6 us (21%)
  Pallas kernels  33.6 us (16%)
  other arithmetic  19.5 us (9%)
  between operations  6.67 us (3%)
  local copies, waits for them, and re-layouts  4.76 us (2%)
    ppermute x8, waiting for transfers between devices, padded(): lax.ppermute(lax.slice_in_dim(block, block.shape[dim] - width, None, axis...  50.7 us
    ppermute x8, waiting for transfers between devices, padded(): lax.ppermute(lax.slice_in_dim(block, 0, width, axis=dim), axis, backward)  43.6 us
    pallas_call x1, Pallas kernels, reconstruct(): pl.pallas_call(shrink_kernel, grid_spec=pltpu.PrefetchScalarGridSpec(num_...  33.6 us
    ppermute x8, starting transfers between devices, padded(): lax.ppermute(lax.slice_in_dim(block, block.shape[dim] - width, None, axis...  32.5 us
    ppermute x8, starting transfers between devices, padded(): lax.ppermute(lax.slice_in_dim(block, 0, width, axis=dim), axis, backward)  10.5 us
    concatenate x4, other arithmetic, padded(): block = jnp.concatenate([low, block, high], axis=dim)  4.66 us
  transfers between devices with their start and end apart: 18, of which 13 were waited for; matrix products, arithmetic and copies ran while one was open for 1% of the time, Pallas kernels for 0%

profile of v1, /device:TPU:0, one launch (start us, length us, event | category | flops | bytes accessed | tf_op | source)
XLA Modules:
  0.0 206.3 jit_solution(3994416209519450272)
XLA Ops:
  2.2 5.0 %collective-permute-start.4 = (f32[32,32,32]{2,1,0:T(8,128)S(1)}, f32[32,32,32]{2,1,0:T(8,128)S(1)}, u32[]{:S(2)}, u32[]{:S(2)}) collective-permute-start(f32[32,32,32]{2,1,0:T(8,128)S(1)} %get-tuple-element.19), channel_id=1, source_target_pairs={{0,1},{1,2},{2,3},{4,5},{5,6},{6,7},{8,9},{9,10},{10,11},{12,13},{... | collective-permute-start | bytes 393224 | tf_op jit(solution)/shard_map/ppermute | solution.py:27
  8.5 9.8 %collective-permute-done.4 = f32[32,32,32]{2,1,0:T(8,128)S(1)} collective-permute-done((f32[32,32,32]{2,1,0:T(8,128)S(1)}, f32[32,32,32]{2,1,0:T(8,128)S(1)}, u32[]{:S(2)}, u32[]{:S(2)}) %collective-permute-start.4) | collective-permute-done | bytes 131104 | tf_op jit(solution)/shard_map/ppermute | solution.py:27
  18.3 4.1 %collective-permute-done.5 = f32[32,32,32]{2,1,0:T(8,128)S(1)} collective-permute-done((f32[32,32,32]{2,1,0:T(8,128)S(1)}, f32[32,32,32]{2,1,0:T(8,128)S(1)}, u32[]{:S(2)}, u32[]{:S(2)}) %collective-permute-start.5) | collective-permute-done | bytes 131104 | tf_op jit(solution)/shard_map/ppermute | solution.py:30
  23.1 3.4 %collective-permute-start.6 = (f32[16,32,192]{2,1,0:T(8,128)S(1)}, f32[16,32,192]{2,1,0:T(8,128)S(1)}, u32[]{:S(2)}, u32[]{:S(2)}) collective-permute-start(f32[16,32,192]{2,1,0:T(8,128)S(1)} %get-tuple-element.17), channel_id=1, source_target_pairs={{0,8},{8,16},{16,24},{1,9},{9,17},{17,25},{2,10},{10,18},{18,26},{... | collective-permute-start | bytes 1179656 | tf_op jit(solution)/shard_map/ppermute | solution.py:27
  27.8 8.6 %collective-permute-done.6 = f32[16,32,192]{2,1,0:T(8,128)S(1)} collective-permute-done((f32[16,32,192]{2,1,0:T(8,128)S(1)}, f32[16,32,192]{2,1,0:T(8,128)S(1)}, u32[]{:S(2)}, u32[]{:S(2)}) %collective-permute-start.6) | collective-permute-done | bytes 393248 | tf_op jit(solution)/shard_map/ppermute | solution.py:27
  36.4 13.2 %collective-permute-done.7 = f32[16,32,192]{2,1,0:T(8,128)S(1)} collective-permute-done((f32[16,32,192]{2,1,0:T(8,128)S(1)}, f32[16,32,192]{2,1,0:T(8,128)S(1)}, u32[]{:S(2)}, u32[]{:S(2)}) %collective-permute-start.7) | collective-permute-done | bytes 393248 | tf_op jit(solution)/shard_map/ppermute | solution.py:30
  53.0 3.4 %collective-permute-start = (bf16[16,32]{1,0:T(8,128)(2,1)S(1)}, bf16[16,32]{1,0:T(8,128)(2,1)S(1)}, u32[]{:S(2)}, u32[]{:S(2)}) collective-permute-start(bf16[16,32]{1,0:T(8,128)(2,1)S(1)} %get-tuple-element.25), channel_id=1, source_target_pairs={{0,8},{8,16},{16,24},{1,9},{9,17},{17,25},{2,10},{10,18},{18,26},{... | collective-permute-start | bytes 3080 | tf_op jit(solution)/shard_map/ppermute | solution.py:27
  57.7 4.2 %collective-permute-done.1 = bf16[16,32]{1,0:T(8,128)(2,1)S(1)} collective-permute-done((bf16[16,32]{1,0:T(8,128)(2,1)S(1)}, bf16[16,32]{1,0:T(8,128)(2,1)S(1)}, u32[]{:S(2)}, u32[]{:S(2)}) %collective-permute-start.1) | collective-permute-done | bytes 1056 | tf_op jit(solution)/shard_map/ppermute | solution.py:30
  62.0 1.7 collective-permute-start.2
  65.0 1.8 collective-permute-done.3
  66.8 3.3 %maximum_select_fusion = f32[64,64,192]{2,1,0:T(8,128)S(1)} fusion(f32[64,16,192]{2,1,0:T(8,128)S(1)} %collective-permute-done.9, f32[16,32,192]{2,1,0:T(8,128)S(1)} %collective-permute-done.7, f32[32,32,32]{2,1,0:T(8,128)S(1)} %collective-permute-done.5, f32[32,32,128]{2,1,0:T(8,128)S(1)} %broadcast_multiply_fusion, ...), kind=kLoop, calls=%fused_computation.6 | loop fusion | flops 5505024 | bytes 6295552 | tf_op jit(solution)/shard_map/jit(_where)/select_n | solution.py:207
  70.2 2.1 %fusion.12 = (f32[64,64,128]{2,1,0:T(8,128)}, f32[64,64,128]{2,1,0:T(8,128)S(1)}) fusion(f32[64,64,192]{2,1,0:T(8,128)S(1)} %maximum_select_fusion), kind=kLoop, calls=%fused_computation.40 | loop fusion | bytes 8388608 | tf_op jit(solution)/shard_map/slice | solution.py:216
  80.2 1.9 select_bitcast_fusion
  83.4 33.6 %shrink.1 = f32[2,4096,128]{2,1,0:T(8,128)S(1)} custom-call(s32[2]{0:T(128)S(1)} %pad_add_fusion.1.counts, s32[4]{0:T(128)S(1)} %copy-done.6, f32[2,4096,128]{2,1,0:T(8,128)S(1)} %pad_maximum_fusion.1.window, bf16[64,192]{1,0:T(8,128)(2,1)S(1)} %copy-done.5, bf16[64,192]{1,0:T(8,128)(2,1)S(1)} %copy-done.4, bf16[256,256]{1,0:T(8,128)(2,1)S(1)} %copy-done.1, ...), custom_call_target="tpu_custom_call" | custom-call | tf_op jit(solution)/shard_map/shrink/pallas_call | solution.py:176
  117.8 3.8 %collective-permute-done.11 = f32[4096,128]{1,0:T(8,128)S(1)} collective-permute-done((f32[4096,128]{1,0:T(8,128)S(1)}, f32[4096,128]{1,0:T(8,128)S(1)}, u32[]{:S(2)}, u32[]{:S(2)}) %collective-permute-start.11) | collective-permute-done | bytes 2097184 | tf_op jit(solution)/shard_map/ppermute | solution.py:36
  126.2 20.7 %collective-permute-done.12 = f32[16,64,192]{2,1,0:T(8,128)S(1)} collective-permute-done((f32[16,64,192]{2,1,0:T(8,128)S(1)}, f32[16,64,192]{2,1,0:T(8,128)S(1)}, u32[]{:S(2)}, u32[]{:S(2)}) %collective-permute-start.12) | collective-permute-done | bytes 786464 | tf_op jit(solution)/shard_map/ppermute | solution.py:27
  146.9 13.8 %collective-permute-done.13 = f32[16,64,192]{2,1,0:T(8,128)S(1)} collective-permute-done((f32[16,64,192]{2,1,0:T(8,128)S(1)}, f32[16,64,192]{2,1,0:T(8,128)S(1)}, u32[]{:S(2)}, u32[]{:S(2)}) %collective-permute-start.13) | collective-permute-done | bytes 786464 | tf_op jit(solution)/shard_map/ppermute | solution.py:30
  161.1 1.9 collective-permute-start.14
  165.9 2.4 %collective-permute-done.15 = f32[96,16,192]{2,1,0:T(8,128)S(1)} collective-permute-done((f32[96,16,192]{2,1,0:T(8,128)S(1)}, f32[96,16,192]{2,1,0:T(8,128)S(1)}, u32[]{:S(2)}, u32[]{:S(2)}) %collective-permute-start.15) | collective-permute-done | bytes 1179680 | tf_op jit(solution)/shard_map/ppermute | solution.py:30
  168.3 3.7 %pad_maximum_fusion = f32[96,96,192]{2,1,0:T(8,128)S(1)} fusion(f32[96,16,192]{2,1,0:T(8,128)S(1)} %collective-permute-done.15, f32[16,64,192]{2,1,0:T(8,128)S(1)} %collective-permute-done.13, f32[64,64,192]{2,1,0:T(8,128)S(1)} %pad_add_fusion, f32[16,64,192]{2,1,0:T(8,128)S(1)} %collective-permute-done.12, f32[96,16,192]{2,1,0:T(8,128)S(1)} %collective-permute-done.14), kind=kLoop, calls=%fused_computation | loop fusion | flops 7077888 | bytes 14155776 | tf_op jit(solution)/shard_map/concatenate | solution.py:31
  171.9 2.6 %fusion = f32[32,96,192]{2,1,0:T(8,128)S(1)} fusion(f32[96,16,192]{2,1,0:T(8,128)S(1)} %collective-permute-done.15, f32[96,16,192]{2,1,0:T(8,128)S(1)} %collective-permute-done.14, f32[16,64,192]{2,1,0:T(8,128)S(1)} %collective-permute-done.13, f32[64,64,192]{2,1,0:T(8,128)S(1)} %pad_add_fusion, f32[16,64,192]{2,1,0:T(8,128)S(1)} %collective-permute-done.12, ...), kind=kLoop, calls=%fused_computation.9 | loop fusion | flops 7667712 | bytes 14155808 | tf_op jit(solution)/shard_map/add | solution.py:199
  175.1 14.5 %collective-permute-start.16 = (f32[32,32,32]{2,1,0:T(8,128)S(1)}, f32[32,32,32]{2,1,0:T(8,128)S(1)}, u32[]{:S(2)}, u32[]{:S(2)}) collective-permute-start(f32[32,32,32]{2,1,0:T(8,128)S(1)} %get-tuple-element.15), channel_id=1, source_target_pairs={{0,1},{1,2},{2,3},{4,5},{5,6},{6,7},{8,9},{9,10},{10,11},{12,13},{... | collective-permute-start | bytes 393224 | tf_op jit(solution)/shard_map/ppermute | solution.py:27
  190.9 10.1 %collective-permute-done.16 = f32[32,32,32]{2,1,0:T(8,128)S(1)} collective-permute-done((f32[32,32,32]{2,1,0:T(8,128)S(1)}, f32[32,32,32]{2,1,0:T(8,128)S(1)}, u32[]{:S(2)}, u32[]{:S(2)}) %collective-permute-start.16) | collective-permute-done | bytes 131104 | tf_op jit(solution)/shard_map/ppermute | solution.py:27
  201.0 4.1 %collective-permute-done.17 = f32[32,32,32]{2,1,0:T(8,128)S(1)} collective-permute-done((f32[32,32,32]{2,1,0:T(8,128)S(1)}, f32[32,32,32]{2,1,0:T(8,128)S(1)}, u32[]{:S(2)}, u32[]{:S(2)}) %collective-permute-start.17) | collective-permute-done | bytes 131104 | tf_op jit(solution)/shard_map/ppermute | solution.py:30
  (62 shorter events, 25.9 us)
Async XLA Ops:
  2.2 16.1 %collective-permute-start.4 = (f32[32,32,32]{2,1,0:T(8,128)S(1)}, f32[32,32,32]{2,1,0:T(8,128)S(1)}, u32[]{:S(2)}, u32[]{:S(2)}) collective-permute-start(f32[32,32,32]{2,1,0:T(8,128)S(1)} %get-tuple-element.19), channel_id=1, source_target_pairs={{0,1},{1,2},{2,3},{4,5},{5,6},{6,7},{8,9},{9,10},{10,11},{12,13},{... | collective-permute-start | bytes 393224 | tf_op jit(solution)/shard_map/ppermute | solution.py:27
  7.2 15.3 %collective-permute-start.5 = (f32[32,32,32]{2,1,0:T(8,128)S(1)}, f32[32,32,32]{2,1,0:T(8,128)S(1)}, u32[]{:S(2)}, u32[]{:S(2)}) collective-permute-start(f32[32,32,32]{2,1,0:T(8,128)S(1)} %get-tuple-element.20), channel_id=1, source_target_pairs={{1,0},{2,1},{3,2},{5,4},{6,5},{7,6},{9,8},{10,9},{11,10},{13,12},{... | collective-permute-start | bytes 393224 | tf_op jit(solution)/shard_map/ppermute | solution.py:30
  23.1 13.4 %collective-permute-start.6 = (f32[16,32,192]{2,1,0:T(8,128)S(1)}, f32[16,32,192]{2,1,0:T(8,128)S(1)}, u32[]{:S(2)}, u32[]{:S(2)}) collective-permute-start(f32[16,32,192]{2,1,0:T(8,128)S(1)} %get-tuple-element.17), channel_id=1, source_target_pairs={{0,8},{8,16},{16,24},{1,9},{9,17},{17,25},{2,10},{10,18},{18,26},{... | collective-permute-start | bytes 1179656 | tf_op jit(solution)/shard_map/ppermute | solution.py:27
  26.5 23.1 %collective-permute-start.7 = (f32[16,32,192]{2,1,0:T(8,128)S(1)}, f32[16,32,192]{2,1,0:T(8,128)S(1)}, u32[]{:S(2)}, u32[]{:S(2)}) collective-permute-start(f32[16,32,192]{2,1,0:T(8,128)S(1)} %get-tuple-element.18), channel_id=1, source_target_pairs={{8,0},{16,8},{24,16},{9,1},{17,9},{25,17},{10,2},{18,10},{26,18},{... | collective-permute-start | bytes 1179656 | tf_op jit(solution)/shard_map/ppermute | solution.py:30
  50.3 16.5 %collective-permute-start.8 = (f32[64,16,192]{2,1,0:T(8,128)S(1)}, f32[64,16,192]{2,1,0:T(8,128)S(1)}, u32[]{:S(2)}, u32[]{:S(2)}) collective-permute-start(f32[64,16,192]{2,1,0:T(8,128)S(1)} %get-tuple-element.13), channel_id=1, source_target_pairs={{0,4},{1,5},{2,6},{3,7},{8,12},{9,13},{10,14},{11,15},{16,20},{17,... | collective-permute-start | bytes 2359304 | tf_op jit(solution)/shard_map/ppermute | solution.py:27
  51.7 15.1 %collective-permute-start.9 = (f32[64,16,192]{2,1,0:T(8,128)S(1)}, f32[64,16,192]{2,1,0:T(8,128)S(1)}, u32[]{:S(2)}, u32[]{:S(2)}) collective-permute-start(f32[64,16,192]{2,1,0:T(8,128)S(1)} %get-tuple-element.14), channel_id=1, source_target_pairs={{4,0},{5,1},{6,2},{7,3},{12,8},{13,9},{14,10},{15,11},{20,16},{21,... | collective-permute-start | bytes 2359304 | tf_op jit(solution)/shard_map/ppermute | solution.py:30
  53.0 4.7 %collective-permute-start = (bf16[16,32]{1,0:T(8,128)(2,1)S(1)}, bf16[16,32]{1,0:T(8,128)(2,1)S(1)}, u32[]{:S(2)}, u32[]{:S(2)}) collective-permute-start(bf16[16,32]{1,0:T(8,128)(2,1)S(1)} %get-tuple-element.25), channel_id=1, source_target_pairs={{0,8},{8,16},{16,24},{1,9},{9,17},{17,25},{2,10},{10,18},{18,26},{... | collective-permute-start | bytes 3080 | tf_op jit(solution)/shard_map/ppermute | solution.py:27
  56.4 5.5 %collective-permute-start.1 = (bf16[16,32]{1,0:T(8,128)(2,1)S(1)}, bf16[16,32]{1,0:T(8,128)(2,1)S(1)}, u32[]{:S(2)}, u32[]{:S(2)}) collective-permute-start(bf16[16,32]{1,0:T(8,128)(2,1)S(1)} %get-tuple-element.26), channel_id=1, source_target_pairs={{8,0},{16,8},{24,16},{9,1},{17,9},{25,17},{10,2},{18,10},{26,18},{... | collective-permute-start | bytes 3080 | tf_op jit(solution)/shard_map/ppermute | solution.py:30
  62.0 3.0 %collective-permute-start.2 = (bf16[64,16]{1,0:T(8,128)(2,1)S(1)}, bf16[64,16]{1,0:T(8,128)(2,1)S(1)}, u32[]{:S(2)}, u32[]{:S(2)}) collective-permute-start(bf16[64,16]{1,0:T(8,128)(2,1)S(1)} %get-tuple-element.21), channel_id=1, source_target_pairs={{0,4},{1,5},{2,6},{3,7},{8,12},{9,13},{10,14},{11,15},{16,20},{17,... | collective-permute-start | bytes 6152 | tf_op jit(solution)/shard_map/ppermute | solution.py:27
  63.6 3.1 %collective-permute-start.3 = (bf16[64,16]{1,0:T(8,128)(2,1)S(1)}, bf16[64,16]{1,0:T(8,128)(2,1)S(1)}, u32[]{:S(2)}, u32[]{:S(2)}) collective-permute-start(bf16[64,16]{1,0:T(8,128)(2,1)S(1)} %get-tuple-element.22), channel_id=1, source_target_pairs={{4,0},{5,1},{6,2},{7,3},{12,8},{13,9},{14,10},{15,11},{20,16},{21,... | collective-permute-start | bytes 6152 | tf_op jit(solution)/shard_map/ppermute | solution.py:30
  70.2 2.3 %copy-start.9 = (s32[1,2,2]{2,1,0:T(2,128)S(1)}, s32[1,2,2]{2,1,0:T(2,128)}, u32[]{:S(2)}) copy-start(s32[1,2,2]{2,1,0:T(2,128)} %param.12) | copy-start | bytes 52
  72.3 7.8 %collective-permute-start.10 = (f32[4096,128]{1,0:T(8,128)S(1)}, f32[4096,128]{1,0:T(8,128)}, u32[]{:S(2)}, u32[]{:S(2)}) collective-permute-start(f32[4096,128]{1,0:T(8,128)S(1)} %bitcast.21), channel_id=1, source_target_pairs={{0,4},{4,0},{1,5},{5,1},{2,6},{6,2},{3,7},{7,3},{8,12},{12,8},{9,1... | collective-permute-start | bytes 6291464 | tf_op jit(solution)/shard_map/ppermute | solution.py:36
  80.2 2.2 %copy-start.7 = (f32[64,64,128]{2,1,0:T(8,128)S(1)}, f32[64,64,128]{2,1,0:T(8,128)}, u32[]{:S(2)}) copy-start(f32[64,64,128]{2,1,0:T(8,128)} %get-tuple-element.11) | copy-start | bytes 6291460
  82.4 1.0 copy-start.1
  82.4 1.0 copy-start.2
  82.4 1.0 copy-start.3
  117.3 4.2 %collective-permute-start.11 = (f32[4096,128]{1,0:T(8,128)S(1)}, f32[4096,128]{1,0:T(8,128)S(1)}, u32[]{:S(2)}, u32[]{:S(2)}) collective-permute-start(f32[4096,128]{1,0:T(8,128)S(1)} %get-tuple-element.9), channel_id=1, source_target_pairs={{0,4},{4,0},{1,5},{5,1},{2,6},{6,2},{3,7},{7,3},{8,12},{12,8},{9,1... | collective-permute-start | bytes 6291464 | tf_op jit(solution)/shard_map/ppermute | solution.py:36
  122.4 24.5 %collective-permute-start.12 = (f32[16,64,192]{2,1,0:T(8,128)S(1)}, f32[16,64,192]{2,1,0:T(8,128)S(1)}, u32[]{:S(2)}, u32[]{:S(2)}) collective-permute-start(f32[16,64,192]{2,1,0:T(8,128)S(1)} %get-tuple-element.7), channel_id=1, source_target_pairs={{0,8},{8,16},{16,24},{1,9},{9,17},{17,25},{2,10},{10,18},{18,26},{... | collective-permute-start | bytes 2359304 | tf_op jit(solution)/shard_map/ppermute | solution.py:27
  123.8 36.9 %collective-permute-start.13 = (f32[16,64,192]{2,1,0:T(8,128)S(1)}, f32[16,64,192]{2,1,0:T(8,128)S(1)}, u32[]{:S(2)}, u32[]{:S(2)}) collective-permute-start(f32[16,64,192]{2,1,0:T(8,128)S(1)} %get-tuple-element.8), channel_id=1, source_target_pairs={{8,0},{16,8},{24,16},{9,1},{17,9},{25,17},{10,2},{18,10},{26,18},{... | collective-permute-start | bytes 2359304 | tf_op jit(solution)/shard_map/ppermute | solution.py:30
  161.1 4.8 %collective-permute-start.14 = (f32[96,16,192]{2,1,0:T(8,128)S(1)}, f32[96,16,192]{2,1,0:T(8,128)S(1)}, u32[]{:S(2)}, u32[]{:S(2)}) collective-permute-start(f32[96,16,192]{2,1,0:T(8,128)S(1)} %get-tuple-element.5), channel_id=1, source_target_pairs={{0,4},{1,5},{2,6},{3,7},{8,12},{9,13},{10,14},{11,15},{16,20},{17,... | collective-permute-start | bytes 3538952 | tf_op jit(solution)/shard_map/ppermute | solution.py:27
  162.9 9.0 %copy-start.8 = (pred[32]{0:T(512)(128)(4,1)S(1)}, pred[32]{0:T(512)(128)(4,1)}, u32[]{:S(2)}) copy-start(pred[32]{0:T(512)(128)(4,1)} %constant.38.clone.1) | copy-start | bytes 100
  162.9 5.3 %collective-permute-start.15 = (f32[96,16,192]{2,1,0:T(8,128)S(1)}, f32[96,16,192]{2,1,0:T(8,128)S(1)}, u32[]{:S(2)}, u32[]{:S(2)}) collective-permute-start(f32[96,16,192]{2,1,0:T(8,128)S(1)} %get-tuple-element.6), channel_id=1, source_target_pairs={{4,0},{5,1},{6,2},{7,3},{12,8},{13,9},{14,10},{15,11},{20,16},{21,... | collective-permute-start | bytes 3538952 | tf_op jit(solution)/shard_map/ppermute | solution.py:30
  175.1 25.9 %collective-permute-start.16 = (f32[32,32,32]{2,1,0:T(8,128)S(1)}, f32[32,32,32]{2,1,0:T(8,128)S(1)}, u32[]{:S(2)}, u32[]{:S(2)}) collective-permute-start(f32[32,32,32]{2,1,0:T(8,128)S(1)} %get-tuple-element.15), channel_id=1, source_target_pairs={{0,1},{1,2},{2,3},{4,5},{5,6},{6,7},{8,9},{9,10},{10,11},{12,13},{... | collective-permute-start | bytes 393224 | tf_op jit(solution)/shard_map/ppermute | solution.py:27
  189.6 15.6 %collective-permute-start.17 = (f32[32,32,32]{2,1,0:T(8,128)S(1)}, f32[32,32,32]{2,1,0:T(8,128)S(1)}, u32[]{:S(2)}, u32[]{:S(2)}) collective-permute-start(f32[32,32,32]{2,1,0:T(8,128)S(1)} %get-tuple-element.16), channel_id=1, source_target_pairs={{1,0},{2,1},{3,2},{5,4},{6,5},{7,6},{9,8},{10,9},{11,10},{13,12},{... | collective-permute-start | bytes 393224 | tf_op jit(solution)/shard_map/ppermute | solution.py:30
  (4 other events, 3.8 us)

commit v2 on v1

--- a/solution.py
+++ b/solution.py
@@ -13,27 +13,9 @@
 WPD = 2
 HALO = 16
 HALO_T = 32
-CORE_T = 64
 DEAD = 1e30
 PITCH = 72
 GROUP = 16
-
-
-def padded(block, sides, width):
-    for axis, dim in sides:
-        count = lax.axis_size(axis)
-        forward = [(i, i + 1) for i in range(count - 1)]
-        backward = [(target, source) for source, target in forward]
-        low = lax.ppermute(
-            lax.slice_in_dim(block, block.shape[dim] - width, None, axis=dim), axis, forward
-        )
-        high = lax.ppermute(lax.slice_in_dim(block, 0, width, axis=dim), axis, backward)
-        block = jnp.concatenate([low, block, high], axis=dim)
-    return block
-
-
-def from_partner(value, axis, stride):
-    return lax.ppermute(value, axis, [(i, i ^ 1 << stride) for i in range(lax.axis_size(axis))])
 
 
 def cosine_table(order):
@@ -100,7 +82,7 @@
 
 
 def shrink_kernel(
-    counts, levels, window, space_f, space_b, time_f, time_b, plane, lines, out, held
+    counts, places, levels, window, space_f, space_b, time_f, time_b, plane, lines, out, held
 ):
     slot = pl.program_id(0)
     last = counts[slot] - 1
@@ -141,12 +123,12 @@
         @pl.loop(0, WIN // GROUP)
         def _(group):
             first = group * GROUP
-            places = [pl.ds(first + n, WIN, stride=PITCH) for n in range(GROUP)]
-            values = along_rows(space_f[...], [held[p, :] for p in places])
+            rows = [pl.ds(first + n, WIN, stride=PITCH) for n in range(GROUP)]
+            values = along_rows(space_f[...], [held[r, :] for r in rows])
             values = [v - jnp.clip(v, -threshold, threshold) for v in values]
             values = along_rows(space_b[...], values)
             for n in range(GROUP):
-                held[places[n], :] = values[n]
+                held[rows[n], :] = values[n]
 
     @pl.loop(0, last)
     def _(step):
@@ -168,43 +150,366 @@
             out[0, pl.ds(start, WIN), :] = estimates[n] * (plane[...] * weight)
 
 
-def reconstruct(windows, counts, levels):
-    slots = windows.shape[0]
+def reconstruct(windows, counts, places, levels):
+    slots = counts.shape[0]
     fixed = tables()
     whole = [pl.BlockSpec(memory_space=pltpu.VMEM)] * len(fixed)
-    block = pl.BlockSpec((1, WIN * WIN, WIN_T), lambda slot, counts, levels: (slot, 0, 0))
+    shape = (1, WIN * WIN, WIN_T)
+    block = pl.BlockSpec(shape, lambda slot, counts, places, levels: (places[slot], 0, 0))
+    result = pl.BlockSpec(shape, lambda slot, counts, places, levels: (slot, 0, 0))
     return pl.pallas_call(
         shrink_kernel,
         grid_spec=pltpu.PrefetchScalarGridSpec(
-            num_scalar_prefetch=2,
+            num_scalar_prefetch=3,
             grid=(slots,),
             in_specs=[block] + whole,
-            out_specs=block,
+            out_specs=result,
             scratch_shapes=[pltpu.VMEM((WIN * PITCH, WIN_T), jnp.float32)],
         ),
-        out_shape=jax.ShapeDtypeStruct(windows.shape, jnp.float32),
+        out_shape=jax.ShapeDtypeStruct((slots,) + windows.shape[1:], jnp.float32),
         compiler_params=pltpu.CompilerParams(vmem_limit_bytes=40 * 2**20),
         name="shrink",
-    )(counts, levels, windows, *fixed)
-
-
-def fold_margins(block, dim, width):
-    extent = block.shape[dim]
-    inner = extent - 4 * width
-    middle = lax.slice_in_dim(block, 2 * width, 2 * width + inner, axis=dim)
-    lower_rim = lax.slice_in_dim(block, 0, width, axis=dim)
-    upper_rim = lax.slice_in_dim(block, extent - width, extent, axis=dim)
-    lower_pad = [(0, inner - width) if axis_number == dim else (0, 0) for axis_number in range(3)]
-    upper_pad = [(inner - width, 0) if axis_number == dim else (0, 0) for axis_number in range(3)]
-    return middle + jnp.pad(lower_rim, lower_pad) + jnp.pad(upper_rim, upper_pad)
-
-
-def shards(traces, live, counts, levels):
-    live_mask = live.astype(jnp.float32)
-    timed = padded(traces * live_mask[:, :, None], (("ta", 2),), HALO_T)
-    observed = padded(timed, (("il", 0), ("xl", 1)), HALO)
-    live_pad = padded(live.astype(jnp.bfloat16), (("il", 0), ("xl", 1)), HALO).astype(jnp.float32)
-    observed = jnp.where(live_pad[:, :, None] == 0.0, DEAD, observed)
+    )(counts, places, levels, windows, *fixed)
+
+
+class Links:
+    def __init__(self, sizes, send_sems, recv_sems):
+        self.sizes, self.send_sems, self.recv_sems = sizes, send_sems, recv_sems
+        self.me = {axis: lax.axis_index(axis) for axis in sizes}
+        self.used = 0
+
+    def has(self, axis, step):
+        if step > 0:
+            return self.me[axis] < self.sizes[axis] - 1
+        return self.me[axis] > 0
+
+    def barrier(self):
+        barrier = pltpu.get_barrier_semaphore()
+        total = 0
+        for axis in self.sizes:
+            for step in (-1, 1):
+                there = self.has(axis, step)
+                total = total + there.astype(jnp.int32)
+
+                @pl.when(there)
+                def _():
+                    pl.semaphore_signal(
+                        barrier,
+                        inc=1,
+                        device_id={axis: self.me[axis] + step},
+                        device_id_type=pl.DeviceIdType.MESH,
+                    )
+
+        pl.semaphore_wait(barrier, total)
+
+    def copy(self, source, target, axis, index):
+        number = self.used
+        self.used += 1
+        return pltpu.make_async_remote_copy(
+            src_ref=source,
+            dst_ref=target,
+            send_sem=self.send_sems.at[number],
+            recv_sem=self.recv_sems.at[number],
+            device_id={axis: index},
+            device_id_type=pl.DeviceIdType.MESH,
+        )
+
+    def send(self, source, target, axis, step):
+        copy = self.copy(source, target, axis, self.me[axis] + step)
+
+        @pl.when(self.has(axis, step))
+        def _():
+            copy.start()
+
+        return copy, axis, step
+
+    def arrive(self, sent, otherwise=None):
+        copy, axis, step = sent
+        there = self.has(axis, -step)
+
+        @pl.when(there)
+        def _():
+            copy.wait_recv()
+
+        if otherwise is not None:
+
+            @pl.when(jnp.logical_not(there))
+            def _():
+                otherwise()
+
+    def finish(self, sents):
+        for copy, axis, step in sents:
+
+            @pl.when(self.has(axis, step))
+            def _():
+                copy.wait_send()
+
+    def partner(self, source, target):
+        me = self.me["xl"]
+        return self.copy(source, target, "xl", me + 1 - 2 * lax.rem(me, 2))
+
+
+QUARTERS = WIN_T // HALO_T
+UNIT = HALO // QUARTERS
+
+
+def lane_numbers(shape):
+    return lax.broadcasted_iota(jnp.int32, shape, len(shape) - 1)
+
+
+def turned(value, shift):
+    shift = shift % WIN_T
+    return pltpu.roll(value, shift, value.ndim - 1) if shift else value
+
+
+def pieces(parts):
+    for h in range(parts):
+        for q in range(QUARTERS):
+            start = h * HALO + q * UNIT
+            yield h, q, pl.ds(start, UNIT), pl.ds(h * UNIT, UNIT)
+
+
+def in_quarter(lanes, q):
+    return (lanes >= q * HALO_T) & (lanes < (q + 1) * HALO_T)
+
+
+def gather_kernel(sizes, mine, out, raw, early, late, to_next, to_prev, send_sems, recv_sems):
+    links = Links(sizes, send_sems, recv_sems)
+    links.barrier()
+    core_i, core_x, _ = mine.shape
+    inner_x = pl.ds(HALO, core_x)
+    low_i, high_i = pl.ds(0, HALO), pl.ds(HALO + core_i, HALO)
+    sent = []
+
+    def send(*args):
+        sent.append(links.send(*args))
+        return sent[-1]
+
+    raw_up = send(mine.at[pl.ds(core_i - HALO, HALO)], raw.at[low_i, inner_x], "il", 1)
+    raw_down = send(mine.at[pl.ds(0, HALO)], raw.at[high_i, inner_x], "il", -1)
+
+    for h, q, span, row in pieces(core_i // HALO):
+        block = mine[span]
+        lanes = lane_numbers(block.shape)
+        chosen = in_quarter(lanes, q)
+        first = turned(block, q * HALO_T)
+        final = turned(block, q * HALO_T - (WIN_T - HALO_T))
+        to_prev[row] = first if q == 0 else jnp.where(chosen, first, to_prev[row])
+        to_next[row] = final if q == 0 else jnp.where(chosen, final, to_next[row])
+
+    inner_p = pl.ds(UNIT, core_i // QUARTERS)
+    early_in = send(to_next, early.at[inner_p, inner_x], "ta", 1)
+    late_in = send(to_prev, late.at[inner_p, inner_x], "ta", -1)
+    raw[pl.ds(HALO, core_i), inner_x] = mine[...]
+
+    def blank(target, source):
+        def fill():
+            target[inner_p, inner_x] = jnp.where(source[...] == DEAD, DEAD, 0.0)
+
+        return fill
+
+    low_p, high_p = pl.ds(0, UNIT), pl.ds(UNIT + core_i // QUARTERS, UNIT)
+    from_p = pl.ds(core_i // QUARTERS, UNIT)
+    waits = [(raw_up, raw, low_i), (raw_down, raw, high_i)]
+    for arrival, buffer, source in ((early_in, early, to_next), (late_in, late, to_prev)):
+        links.arrive(arrival, blank(buffer, source))
+        up = send(buffer.at[from_p, inner_x], buffer.at[low_p, inner_x], "il", 1)
+        down = send(buffer.at[pl.ds(UNIT, UNIT), inner_x], buffer.at[high_p, inner_x], "il", -1)
+        waits += [(up, buffer, low_p), (down, buffer, high_p)]
+
+    def missing(target, first, second):
+        def fill():
+            shape = target.at[first, second].shape
+            target[first, second] = jnp.full(shape, DEAD, jnp.float32)
+
+        return fill
+
+    for arrival, buffer, place in waits:
+        links.arrive(arrival, missing(buffer, place, inner_x))
+
+    waits = []
+    low_x, high_x = pl.ds(0, HALO), pl.ds(HALO + core_x, HALO)
+    for buffer in (raw, early, late):
+        whole = pl.ds(0, buffer.shape[0])
+        up = send(buffer.at[whole, pl.ds(core_x, HALO)], buffer.at[whole, low_x], "xl", 1)
+        down = send(buffer.at[whole, pl.ds(HALO, HALO)], buffer.at[whole, high_x], "xl", -1)
+        waits += [(up, buffer, low_x), (down, buffer, high_x)]
+    for arrival, buffer, place in waits:
+        links.arrive(arrival, missing(buffer, pl.ds(0, buffer.shape[0]), place))
+
+    for h, q, span, row in pieces(WIN // HALO):
+        block = raw[span]
+        lanes = lane_numbers(block.shape)
+        added = turned(late[row], WIN_T - HALO_T - q * HALO_T)
+        out[1, span] = jnp.where(lanes < WIN_T - HALO_T, turned(block, -HALO_T), added)
+    trade = links.partner(out.at[1], out.at[2])
+    trade.start()
+    for h, q, span, row in pieces(WIN // HALO):
+        block = raw[span]
+        lanes = lane_numbers(block.shape)
+        added = turned(early[row], -q * HALO_T)
+        out[0, span] = jnp.where(lanes < HALO_T, added, turned(block, HALO_T))
+    trade.wait()
+    links.finish(sent)
+
+
+def gather_windows(coded, sizes):
+    packed = (WIN // QUARTERS, WIN, WIN_T)
+    small = (coded.shape[0] // QUARTERS, coded.shape[1], WIN_T)
+    scratch = [(WIN, WIN, WIN_T), packed, packed, small, small]
+    return pl.pallas_call(
+        functools.partial(gather_kernel, sizes),
+        out_shape=jax.ShapeDtypeStruct((3, WIN, WIN, WIN_T), jnp.float32),
+        in_specs=[pl.BlockSpec(memory_space=pltpu.VMEM)],
+        out_specs=pl.BlockSpec(memory_space=pltpu.VMEM),
+        scratch_shapes=[pltpu.VMEM(shape, jnp.float32) for shape in scratch]
+        + [pltpu.SemaphoreType.DMA((15,)), pltpu.SemaphoreType.DMA((15,))],
+        compiler_params=pltpu.CompilerParams(
+            collective_id=0, has_side_effects=True, vmem_limit_bytes=40 * 2**20
+        ),
+        name="gather_windows",
+    )(coded)
+
+
+def scatter_kernel(
+    sizes,
+    flag,
+    done,
+    out,
+    foreign,
+    raw,
+    early,
+    late,
+    side_raw,
+    side_early,
+    side_late,
+    edge_raw,
+    edge_early,
+    edge_late,
+    from_time,
+    send_sems,
+    recv_sems,
+):
+    links = Links(sizes, send_sems, recv_sems)
+    links.barrier()
+    core_i, core_x, _ = out.shape
+    inner_x = pl.ds(HALO, core_x)
+    sent = []
+
+    def send(*args):
+        sent.append(links.send(*args))
+        return sent[-1]
+
+    trade = links.partner(done.at[1], foreign)
+    trade.start()
+    for h, q, span, row in pieces(WIN // HALO):
+        block = done[0, span]
+        lanes = lane_numbers(block.shape)
+        raw[span] = jnp.where(lanes < WIN_T - HALO_T, turned(block, -HALO_T), 0.0)
+        first = turned(block, q * HALO_T)
+        early[row] = first if q == 0 else jnp.where(in_quarter(lanes, q), first, early[row])
+    trade.wait()
+    for h, q, span, row in pieces(WIN // HALO):
+        block = jnp.where(flag[...][None, :1, :] > 0.5, foreign[span], done[1, span])
+        lanes = lane_numbers(block.shape)
+        raw[span] = raw[span] + jnp.where(lanes >= HALO_T, turned(block, HALO_T), 0.0)
+        final = turned(block, q * HALO_T - (WIN_T - HALO_T))
+        late[row] = final if q == 0 else jnp.where(in_quarter(lanes, q), final, late[row])
+
+    def add(target, first, second, source):
+        there = target[first, second]
+        target[first, second] = there + source[...]
+
+    waits = []
+    for buffer, side in ((raw, side_raw), (early, side_early), (late, side_late)):
+        whole = pl.ds(0, buffer.shape[0])
+        down = send(buffer.at[whole, pl.ds(0, HALO)], side.at[0], "xl", -1)
+        up = send(buffer.at[whole, pl.ds(HALO + core_x, HALO)], side.at[1], "xl", 1)
+        waits += [
+            (down, buffer, whole, pl.ds(core_x, HALO), side.at[0]),
+            (up, buffer, whole, pl.ds(HALO, HALO), side.at[1]),
+        ]
+
+    def gathered(waits):
+        for arrival, buffer, first, second, source in waits:
+            links.arrive(arrival)
+            _, axis, step = arrival
+
+            @pl.when(links.has(axis, -step))
+            def _():
+                add(buffer, first, second, source)
+
+    gathered(waits)
+
+    waits = []
+    for buffer, edge, width in (
+        (early, edge_early, UNIT),
+        (late, edge_late, UNIT),
+        (raw, edge_raw, HALO),
+    ):
+        total = buffer.shape[0]
+        inner = total - 2 * width
+        down = send(buffer.at[pl.ds(0, width), inner_x], edge.at[0], "il", -1)
+        up = send(buffer.at[pl.ds(total - width, width), inner_x], edge.at[1], "il", 1)
+        waits += [
+            (down, buffer, pl.ds(inner, width), inner_x, edge.at[0]),
+            (up, buffer, pl.ds(width, width), inner_x, edge.at[1]),
+        ]
+    gathered(waits[:4])
+    inner_p = pl.ds(UNIT, core_i // QUARTERS)
+    back = send(early.at[inner_p, inner_x], from_time.at[0], "ta", -1)
+    ahead = send(late.at[inner_p, inner_x], from_time.at[1], "ta", 1)
+    gathered(waits[4:])
+    out[...] = raw[pl.ds(HALO, core_i), inner_x]
+    for arrival, side, shift in ((back, 0, WIN_T - HALO_T), (ahead, 1, 0)):
+        links.arrive(arrival)
+        _, axis, step = arrival
+
+        @pl.when(links.has(axis, -step))
+        def _():
+            for h, q, span, row in pieces(core_i // HALO):
+                block = turned(from_time[side, row], shift - q * HALO_T)
+                lanes = lane_numbers(block.shape)
+                kept = in_quarter(lanes, shift // HALO_T)
+                out[span] = out[span] + jnp.where(kept, block, 0.0)
+
+    links.finish(sent)
+
+
+def scatter_windows(flag, done, shape, sizes):
+    core_i, core_x, _ = shape
+    packed = (WIN // QUARTERS, WIN, WIN_T)
+    small = (WIN // QUARTERS, HALO, WIN_T)
+    scratch = [
+        (WIN, WIN, WIN_T),
+        (WIN, WIN, WIN_T),
+        packed,
+        packed,
+        (2, WIN, HALO, WIN_T),
+        (2,) + small,
+        (2,) + small,
+        (2, HALO, core_x, WIN_T),
+        (2, UNIT, core_x, WIN_T),
+        (2, UNIT, core_x, WIN_T),
+        (2, core_i // QUARTERS, core_x, WIN_T),
+    ]
+    return pl.pallas_call(
+        functools.partial(scatter_kernel, sizes),
+        out_shape=jax.ShapeDtypeStruct(shape, jnp.float32),
+        in_specs=[pl.BlockSpec(memory_space=pltpu.VMEM)] * 2,
+        out_specs=pl.BlockSpec(memory_space=pltpu.VMEM),
+        scratch_shapes=[pltpu.VMEM(shape, jnp.float32) for shape in scratch]
+        + [pltpu.SemaphoreType.DMA((15,)), pltpu.SemaphoreType.DMA((15,))],
+        compiler_params=pltpu.CompilerParams(
+            collective_id=1, has_side_effects=True, vmem_limit_bytes=40 * 2**20
+        ),
+        name="scatter_windows",
+    )(flag, done)
+
+
+def shards(sizes, traces, live, counts, levels):
+    coded = jnp.where(live[:, :, None] == 0, DEAD, traces)
+    windows = gather_windows(coded, sizes).reshape(3, WIN * WIN, WIN_T)
     position = lax.axis_index("xl")
     line_counts = counts[0]
     own = lax.dynamic_index_in_dim(line_counts, position, 0, keepdims=False)
@@ -212,27 +517,20 @@
     before = jnp.maximum(own[0] + own[1], other[0] + other[1])
     after = jnp.maximum(own[0] + other[1], other[0] + own[1])
     trading = after < before
-    windows = [
-        observed[:, :, slot * CORE_T : slot * CORE_T + WIN_T].reshape(WIN * WIN, WIN_T)
-        for slot in range(WPD)
-    ]
-    arrived = from_partner(windows[1], "xl", 0)
-    windows[1] = jnp.where(trading, arrived, windows[1])
     work = jnp.stack([own[0], jnp.where(trading, other[1], own[1])])
-    done = reconstruct(jnp.stack(windows), work, levels)
-    results = [done[0], jnp.where(trading, from_partner(done[1], "xl", 0), done[1])]
-    results = [r.reshape(WIN, WIN, WIN_T) for r in results]
-    accumulated = jnp.pad(results[0], ((0, 0), (0, 0), (0, CORE_T)))
-    accumulated = accumulated + jnp.pad(results[1], ((0, 0), (0, 0), (CORE_T, 0)))
-    spread = padded(accumulated, (("il", 0), ("xl", 1)), HALO)
-    spread = fold_margins(spread, 0, HALO)
-    spread = fold_margins(spread, 1, HALO)
-    spread = padded(spread, (("ta", 2),), HALO_T)
-    return fold_margins(spread, 2, HALO_T)
+    places = jnp.stack([jnp.int32(0), jnp.where(trading, 2, 1)])
+    done = reconstruct(windows, work, places, levels)
+    flag = jnp.full((8, WIN_T), trading.astype(jnp.float32))
+    return scatter_windows(flag, done.reshape(WPD, WIN, WIN, WIN_T), traces.shape, sizes)
 
 
 def solution(mesh):
     placed = (P("il", "xl", "ta"), P("il", "xl"), P("il", None, "ta"), P())
+    sizes = {axis: mesh.shape[axis] for axis in ("il", "xl", "ta")}
     return jax.shard_map(
-        shards, mesh=mesh, in_specs=placed, out_specs=P("il", "xl", "ta"), check_vma=False
+        functools.partial(shards, sizes),
+        mesh=mesh,
+        in_specs=placed,
+        out_specs=P("il", "xl", "ta"),
+        check_vma=False,
     )

time: 207 us -> 106 us (0.51)
  the two profiles are of different devices: /device:TPU:0 before, /device:TPU:20 now
where the time goes in v2:
time: 106 us; the launch traced here: 105 us
  Pallas kernels  89.5 us (84%)
  between operations  6.49 us (6%)
  local copies, waits for them, and re-layouts  6.42 us (6%)
  other arithmetic  2.74 us (3%)
    pallas_call x1, Pallas kernels, scatter_windows(): pl.pallas_call(functools.partial(scatter_kernel, sizes), out_shape=jax.Sh...  39.4 us
    pallas_call x1, Pallas kernels, gather_windows(): pl.pallas_call(functools.partial(gather_kernel, sizes), out_shape=jax.Sha...  26.9 us
    pallas_call x1, Pallas kernels, reconstruct(): pl.pallas_call(shrink_kernel, grid_spec=pltpu.PrefetchScalarGridSpec(num_...  23.2 us
    unnamed x19, local copies, waits for them, and re-layouts  4.96 us

profile of v2, /device:TPU:20, one launch (start us, length us, event | category | flops | bytes accessed | tf_op | source)
XLA Modules:
  0.0 105.2 jit_solution(6583795519328929042)
XLA Ops:
  0.0 0.0 copy-start.3
  0.0 0.0 copy-start.6
  0.0 0.0 copy-start.7
  0.0 0.0 copy-start.8
  0.1 0.8 constant_dynamic-slice_fusion
  0.9 0.7 fusion
  7.9 0.7 pad_add_fusion.counts
  8.6 0.1 pad_add_fusion.1.places
  8.7 0.7 broadcast_compare_fusion
  9.4 1.2 %broadcast_select_fusion.mine = f32[32,32,128]{2,1,0:T(8,128)S(1)} fusion(f32[32,32,128]{2,1,0:T(8,128)} %param.10, pred[32,32]{1,0:T(8,128)(4,1)S(1)} %broadcast_compare_fusion), kind=kLoop, calls=%fused_computation | loop fusion | flops 131072 | bytes 1049600 | tf_op jit(solution)/shard_map/jit(_where)/select_n | solution.py:511
  10.6 26.9 %gather_windows.1 = f32[3,64,64,128]{3,2,1,0:T(8,128)S(1)} custom-call(f32[32,32,128]{2,1,0:T(8,128)S(1)} %broadcast_select_fusion.mine), custom_call_target="tpu_custom_call" | custom-call | tf_op jit(solution)/shard_map/gather_windows/pallas_call | solution.py:360
  37.5 0.0 copy-done.4
  37.5 0.0 copy-done.5
  37.5 0.0 copy-done.2
  37.5 0.0 copy-done.3
  37.6 0.0 copy-done.6
  37.6 0.0 copy-done.7
  37.6 0.0 copy-done.8
  37.6 23.2 %shrink.1 = f32[2,4096,128]{2,1,0:T(8,128)S(1)} custom-call(s32[2]{0:T(128)S(1)} %pad_add_fusion.counts, s32[2]{0:T(128)S(1)} %pad_add_fusion.1.places, s32[4]{0:T(128)S(1)} %copy-done.8, f32[3,4096,128]{2,1,0:T(8,128)S(1)} %bitcast.9, bf16[64,192]{1,0:T(8,128)(2,1)S(1)} %copy-done.4, bf16[64,192]{1,0:T(8,128)(2,1)S(1)} %copy-done.5, ...), custom_call_target="tpu_custom_call" | custom-call | tf_op jit(solution)/shard_map/shrink/pallas_call | solution.py:160
  60.8 0.0 copy-start
  60.8 1.9 %copy-done = f32[2,4096,128]{2,1,0:T(8,128)} copy-done((f32[2,4096,128]{2,1,0:T(8,128)}, f32[2,4096,128]{2,1,0:T(8,128)S(1)}, u32[]{:S(2)}) %copy-start) | copy-done | bytes 4194328
  62.8 2.2 %copy-done.1 = f32[2,4096,128]{2,1,0:T(8,128)S(1)} copy-done((f32[2,4096,128]{2,1,0:T(8,128)S(1)}, f32[2,4096,128]{2,1,0:T(8,128)}, u32[]{:S(2)}) %copy-start.1) | copy-done | bytes 4194328
  65.0 39.4 %scatter_windows.1 = f32[32,32,128]{2,1,0:T(8,128)S(1)} custom-call(f32[8,128]{1,0:T(8,128)S(1)} %broadcast_in_dim.16.flag, f32[2,64,64,128]{3,2,1,0:T(8,128)S(1)} %bitcast.10), custom_call_target="tpu_custom_call" | custom-call | tf_op jit(solution)/shard_map/scatter_windows/pallas_call | solution.py:496
  104.4 0.8 copy.12
  (5 shorter events, 0.0 us)
Async XLA Ops:
  0.0 37.5 %copy-start.4 = (bf16[64,192]{1,0:T(8,128)(2,1)S(1)}, bf16[64,192]{1,0:T(8,128)(2,1)}, u32[]{:S(2)}) copy-start(bf16[64,192]{1,0:T(8,128)(2,1)} %constant.36.clone.space_f) | copy-start | bytes 73732
  0.0 37.5 %copy-start.5 = (bf16[64,192]{1,0:T(8,128)(2,1)S(1)}, bf16[64,192]{1,0:T(8,128)(2,1)}, u32[]{:S(2)}) copy-start(bf16[64,192]{1,0:T(8,128)(2,1)} %constant.37.clone.space_b) | copy-start | bytes 73732
  0.0 37.5 %copy-start.2 = (bf16[256,256]{1,0:T(8,128)(2,1)S(1)}, bf16[256,256]{1,0:T(8,128)(2,1)}, u32[]{:S(2)}) copy-start(bf16[256,256]{1,0:T(8,128)(2,1)} %constant.38.clone.time_f) | copy-start | bytes 393220
  0.0 37.5 %copy-start.3 = (bf16[256,256]{1,0:T(8,128)(2,1)S(1)}, bf16[256,256]{1,0:T(8,128)(2,1)}, u32[]{:S(2)}) copy-start(bf16[256,256]{1,0:T(8,128)(2,1)} %constant.39.clone.time_b) | copy-start | bytes 393220
  0.0 37.5 %copy-start.6 = (f32[64,128]{1,0:T(8,128)S(1)}, f32[64,128]{1,0:T(8,128)}, u32[]{:S(2)}) copy-start(f32[64,128]{1,0:T(8,128)} %constant.40.clone.plane) | copy-start | bytes 98308
  0.0 37.5 %copy-start.7 = (f32[64,128]{1,0:T(8,128)S(1)}, f32[64,128]{1,0:T(8,128)}, u32[]{:S(2)}) copy-start(f32[64,128]{1,0:T(8,128)} %constant.41.clone.lines) | copy-start | bytes 98308
  0.0 37.5 %copy-start.8 = (s32[4]{0:T(128)S(1)}, s32[4]{0:T(128)}, u32[]{:S(2)}) copy-start(s32[4]{0:T(128)} %levels.1) | copy-start | bytes 52
  60.8 1.9 %copy-start = (f32[2,4096,128]{2,1,0:T(8,128)}, f32[2,4096,128]{2,1,0:T(8,128)S(1)}, u32[]{:S(2)}) copy-start(f32[2,4096,128]{2,1,0:T(8,128)S(1)} %shrink.1) | copy-start | bytes 12582916
  62.8 2.2 %copy-start.1 = (f32[2,4096,128]{2,1,0:T(8,128)S(1)}, f32[2,4096,128]{2,1,0:T(8,128)}, u32[]{:S(2)}) copy-start(f32[2,4096,128]{2,1,0:T(8,128)} %copy-done) | copy-start | bytes 12582916

commit v3 on v2

--- a/solution.py
+++ b/solution.py
@@ -41,7 +41,8 @@
     space = cosine_table(WIN)
     for table in (space, space.T):
         high, low = halves(table)
-        out.append(np.concatenate([high, high, low], axis=1))
+        upper = np.concatenate([high, high], axis=1)
+        out.append(np.concatenate([upper, np.concatenate([low, 0 * low], axis=1)], axis=0))
     time = cosine_table(WIN_T)
     for table in (time.T, time):
         high, low = halves(table)
@@ -66,8 +67,9 @@
     for n in range(0, len(slices), 2):
         high, low = split(jnp.concatenate([slices[n], slices[n + 1]], axis=1))
         both = jnp.dot(
-            table, jnp.concatenate([high, low, high], axis=0), preferred_element_type=jnp.float32
+            table, jnp.concatenate([high, low], axis=0), preferred_element_type=jnp.float32
         )
+        both = both[:WIN] + both[WIN:]
         out += [both[:, :WIN_T], both[:, WIN_T:]]
     return out
 
@@ -82,10 +84,52 @@
 
 
 def shrink_kernel(
-    counts, places, levels, window, space_f, space_b, time_f, time_b, plane, lines, out, held
+    counts,
+    levels,
+    windows,
+    space_f,
+    space_b,
+    time_f,
+    time_b,
+    plane,
+    lines,
+    out,
+    flag,
+    held,
+    window,
+    ready,
+    in_sems,
+    out_sems,
 ):
-    slot = pl.program_id(0)
-    last = counts[slot] - 1
+    me = lax.axis_index("xl")
+    other = me + 1 - 2 * lax.rem(me, 2)
+    own_first, own_final = counts[WPD * me], counts[WPD * me + 1]
+    other_first, other_final = counts[WPD * other], counts[WPD * other + 1]
+    before = jnp.maximum(own_first + own_final, other_first + other_final)
+    after = jnp.maximum(own_first + other_final, other_first + own_final)
+    trading = after < before
+    flag[...] = jnp.full(flag.shape, jnp.where(trading, 1.0, 0.0), jnp.float32)
+    second = jnp.where(trading, 2, 1)
+    pltpu.make_async_copy(windows.at[0], window.at[0], in_sems.at[0]).start()
+    pltpu.make_async_copy(windows.at[second], window.at[1], in_sems.at[1]).start()
+
+    @pl.loop(0, WPD)
+    def _(slot):
+        pltpu.make_async_copy(windows.at[slot], window.at[slot], in_sems.at[slot]).wait()
+        final = jnp.where(trading, other_final, own_final)
+        count = jnp.where(slot == 0, own_first, final)
+        tables = (space_f, space_b, time_f, time_b, plane, lines)
+        shrink_window(count, levels, window.at[slot], *tables, ready.at[slot], held)
+        pltpu.make_async_copy(ready.at[slot], out.at[slot], out_sems.at[slot]).start()
+
+    for slot in range(WPD):
+        pltpu.make_async_copy(ready.at[slot], out.at[slot], out_sems.at[slot]).wait()
+
+
+def shrink_window(
+    count, levels, window, space_f, space_b, time_f, time_b, plane, lines, out, held
+):
+    last = count - 1
 
     def forward(group, estimates):
         done = along_rows(space_f[...], along_lanes(time_f[...], estimates))
@@ -95,7 +139,7 @@
 
     def recorded(group, n):
         start = pl.multiple_of((group * GROUP + n) * WIN, 8)
-        return window[0, pl.ds(start, WIN), :]
+        return window[pl.ds(start, WIN), :]
 
     def backward(group):
         slices = []
@@ -147,29 +191,33 @@
             line = group * GROUP + n
             start = pl.multiple_of(line * WIN, 8)
             weight = lines[pl.ds(line, 1), :]
-            out[0, pl.ds(start, WIN), :] = estimates[n] * (plane[...] * weight)
-
-
-def reconstruct(windows, counts, places, levels):
-    slots = counts.shape[0]
+            out[pl.ds(start, WIN), :] = estimates[n] * (plane[...] * weight)
+
+
+def reconstruct(windows, counts, levels):
     fixed = tables()
-    whole = [pl.BlockSpec(memory_space=pltpu.VMEM)] * len(fixed)
-    shape = (1, WIN * WIN, WIN_T)
-    block = pl.BlockSpec(shape, lambda slot, counts, places, levels: (places[slot], 0, 0))
-    result = pl.BlockSpec(shape, lambda slot, counts, places, levels: (slot, 0, 0))
+    shape = (WPD,) + windows.shape[1:]
+    vmem = pl.BlockSpec(memory_space=pltpu.VMEM)
+    smem = pl.BlockSpec(memory_space=pltpu.SMEM)
+    hbm = pl.BlockSpec(memory_space=pl.ANY)
     return pl.pallas_call(
         shrink_kernel,
-        grid_spec=pltpu.PrefetchScalarGridSpec(
-            num_scalar_prefetch=3,
-            grid=(slots,),
-            in_specs=[block] + whole,
-            out_specs=result,
-            scratch_shapes=[pltpu.VMEM((WIN * PITCH, WIN_T), jnp.float32)],
-        ),
-        out_shape=jax.ShapeDtypeStruct((slots,) + windows.shape[1:], jnp.float32),
+        in_specs=[smem, smem, hbm] + [vmem] * len(fixed),
+        out_specs=[hbm, vmem],
+        out_shape=[
+            jax.ShapeDtypeStruct(shape, jnp.float32),
+            jax.ShapeDtypeStruct((8, WIN_T), jnp.float32),
+        ],
+        scratch_shapes=[
+            pltpu.VMEM((WIN * PITCH, WIN_T), jnp.float32),
+            pltpu.VMEM(shape, jnp.float32),
+            pltpu.VMEM(shape, jnp.float32),
+            pltpu.SemaphoreType.DMA((WPD,)),
+            pltpu.SemaphoreType.DMA((WPD,)),
+        ],
         compiler_params=pltpu.CompilerParams(vmem_limit_bytes=40 * 2**20),
         name="shrink",
-    )(counts, places, levels, windows, *fixed)
+    )(counts, levels, windows, *fixed)
 
 
 class Links:
@@ -273,10 +321,32 @@
     return (lanes >= q * HALO_T) & (lanes < (q + 1) * HALO_T)
 
 
-def gather_kernel(sizes, mine, out, raw, early, late, to_next, to_prev, send_sems, recv_sems):
+def gather_kernel(
+    sizes,
+    traces,
+    live,
+    out,
+    mine,
+    raw,
+    early,
+    late,
+    to_next,
+    to_prev,
+    ready,
+    local_sems,
+    send_sems,
+    recv_sems,
+):
     links = Links(sizes, send_sems, recv_sems)
+    core_i, core_x, _ = mine.shape
+    square = (core_x, core_x)
+    same = lax.broadcasted_iota(jnp.int32, square, 0) == lax.broadcasted_iota(jnp.int32, square, 1)
+    spread = [jnp.where(same, live[pl.ds(n, 1), :], 0) for n in range(core_i)]
+    spread = jnp.concatenate(spread, axis=0).astype(jnp.float32).astype(jnp.bfloat16)
+    ones = jnp.ones((core_x, WIN_T), jnp.bfloat16)
+    seen = jnp.dot(spread, ones, preferred_element_type=jnp.float32).reshape(mine.shape)
+    mine[...] = jnp.where(seen > 0.5, traces[...], DEAD)
     links.barrier()
-    core_i, core_x, _ = mine.shape
     inner_x = pl.ds(HALO, core_x)
     low_i, high_i = pl.ds(0, HALO), pl.ds(HALO + core_i, HALO)
     sent = []
@@ -341,41 +411,48 @@
         block = raw[span]
         lanes = lane_numbers(block.shape)
         added = turned(late[row], WIN_T - HALO_T - q * HALO_T)
-        out[1, span] = jnp.where(lanes < WIN_T - HALO_T, turned(block, -HALO_T), added)
-    trade = links.partner(out.at[1], out.at[2])
+        ready[1, span] = jnp.where(lanes < WIN_T - HALO_T, turned(block, -HALO_T), added)
+    trade = links.partner(ready.at[1], out.at[2])
     trade.start()
+    keep = [pltpu.make_async_copy(ready.at[n], out.at[n], local_sems.at[n]) for n in range(WPD)]
+    keep[1].start()
     for h, q, span, row in pieces(WIN // HALO):
         block = raw[span]
         lanes = lane_numbers(block.shape)
         added = turned(early[row], -q * HALO_T)
-        out[0, span] = jnp.where(lanes < HALO_T, added, turned(block, HALO_T))
+        ready[0, span] = jnp.where(lanes < HALO_T, added, turned(block, HALO_T))
+    keep[0].start()
+    keep[0].wait()
+    keep[1].wait()
     trade.wait()
     links.finish(sent)
 
 
-def gather_windows(coded, sizes):
+def gather_windows(traces, live, sizes):
     packed = (WIN // QUARTERS, WIN, WIN_T)
-    small = (coded.shape[0] // QUARTERS, coded.shape[1], WIN_T)
-    scratch = [(WIN, WIN, WIN_T), packed, packed, small, small]
+    small = (traces.shape[0] // QUARTERS, traces.shape[1], WIN_T)
+    scratch = [traces.shape, (WIN, WIN, WIN_T), packed, packed, small, small]
+    scratch += [(WPD, WIN, WIN, WIN_T)]
     return pl.pallas_call(
         functools.partial(gather_kernel, sizes),
         out_shape=jax.ShapeDtypeStruct((3, WIN, WIN, WIN_T), jnp.float32),
-        in_specs=[pl.BlockSpec(memory_space=pltpu.VMEM)],
-        out_specs=pl.BlockSpec(memory_space=pltpu.VMEM),
+        in_specs=[pl.BlockSpec(memory_space=pltpu.VMEM)] * 2,
+        out_specs=pl.BlockSpec(memory_space=pl.ANY),
         scratch_shapes=[pltpu.VMEM(shape, jnp.float32) for shape in scratch]
-        + [pltpu.SemaphoreType.DMA((15,)), pltpu.SemaphoreType.DMA((15,))],
+        + [pltpu.SemaphoreType.DMA((WPD,)), pltpu.SemaphoreType.DMA((15,)), pltpu.SemaphoreType.DMA((15,))],
         compiler_params=pltpu.CompilerParams(
             collective_id=0, has_side_effects=True, vmem_limit_bytes=40 * 2**20
         ),
         name="gather_windows",
-    )(coded)
+    )(traces, live)
 
 
 def scatter_kernel(
     sizes,
     flag,
+    results,
+    out,
     done,
-    out,
     foreign,
     raw,
     early,
@@ -387,10 +464,16 @@
     edge_early,
     edge_late,
     from_time,
+    local_sems,
     send_sems,
     recv_sems,
 ):
     links = Links(sizes, send_sems, recv_sems)
+    loads = [
+        pltpu.make_async_copy(results.at[n], done.at[n], local_sems.at[n]) for n in range(WPD)
+    ]
+    for load in loads:
+        load.start()
     links.barrier()
     core_i, core_x, _ = out.shape
     inner_x = pl.ds(HALO, core_x)
@@ -400,8 +483,10 @@
         sent.append(links.send(*args))
         return sent[-1]
 
-    trade = links.partner(done.at[1], foreign)
+    trade = links.partner(results.at[1], foreign)
     trade.start()
+    for load in loads:
+        load.wait()
     for h, q, span, row in pieces(WIN // HALO):
         block = done[0, span]
         lanes = lane_numbers(block.shape)
@@ -481,6 +566,7 @@
     packed = (WIN // QUARTERS, WIN, WIN_T)
     small = (WIN // QUARTERS, HALO, WIN_T)
     scratch = [
+        (WPD, WIN, WIN, WIN_T),
         (WIN, WIN, WIN_T),
         (WIN, WIN, WIN_T),
         packed,
@@ -496,10 +582,10 @@
     return pl.pallas_call(
         functools.partial(scatter_kernel, sizes),
         out_shape=jax.ShapeDtypeStruct(shape, jnp.float32),
-        in_specs=[pl.BlockSpec(memory_space=pltpu.VMEM)] * 2,
+        in_specs=[pl.BlockSpec(memory_space=pltpu.VMEM), pl.BlockSpec(memory_space=pl.ANY)],
         out_specs=pl.BlockSpec(memory_space=pltpu.VMEM),
         scratch_shapes=[pltpu.VMEM(shape, jnp.float32) for shape in scratch]
-        + [pltpu.SemaphoreType.DMA((15,)), pltpu.SemaphoreType.DMA((15,))],
+        + [pltpu.SemaphoreType.DMA((WPD,)), pltpu.SemaphoreType.DMA((15,)), pltpu.SemaphoreType.DMA((15,))],
         compiler_params=pltpu.CompilerParams(
             collective_id=1, has_side_effects=True, vmem_limit_bytes=40 * 2**20
         ),
@@ -508,19 +594,8 @@
 
 
 def shards(sizes, traces, live, counts, levels):
-    coded = jnp.where(live[:, :, None] == 0, DEAD, traces)
-    windows = gather_windows(coded, sizes).reshape(3, WIN * WIN, WIN_T)
-    position = lax.axis_index("xl")
-    line_counts = counts[0]
-    own = lax.dynamic_index_in_dim(line_counts, position, 0, keepdims=False)
-    other = lax.dynamic_index_in_dim(line_counts, jnp.bitwise_xor(position, 1), 0, keepdims=False)
-    before = jnp.maximum(own[0] + own[1], other[0] + other[1])
-    after = jnp.maximum(own[0] + other[1], other[0] + own[1])
-    trading = after < before
-    work = jnp.stack([own[0], jnp.where(trading, other[1], own[1])])
-    places = jnp.stack([jnp.int32(0), jnp.where(trading, 2, 1)])
-    done = reconstruct(windows, work, places, levels)
-    flag = jnp.full((8, WIN_T), trading.astype(jnp.float32))
+    windows = gather_windows(traces, live, sizes).reshape(3, WIN * WIN, WIN_T)
+    done, flag = reconstruct(windows, counts.reshape(-1), levels)
     return scatter_windows(flag, done.reshape(WPD, WIN, WIN, WIN_T), traces.shape, sizes)
 
 

time: 106 us -> 95.7 us (0.903)
  the two profiles are of different devices: /device:TPU:20 before, /device:TPU:12 now
where the time goes in v3:
time: 95.7 us; the launch traced here: 95.3 us
  Pallas kernels  91.9 us (96%)
  local copies, waits for them, and re-layouts  3.36 us (4%)
    pallas_call x1, Pallas kernels, scatter_windows(): pl.pallas_call(functools.partial(scatter_kernel, sizes), out_shape=jax.Sh...  40.1 us
    pallas_call x1, Pallas kernels, gather_windows(): pl.pallas_call(functools.partial(gather_kernel, sizes), out_shape=jax.Sha...  27.1 us
    pallas_call x1, Pallas kernels, reconstruct(): pl.pallas_call(shrink_kernel, in_specs=[smem, smem, hbm] + [vmem] * len(f...  24.7 us
    unnamed x19, local copies, waits for them, and re-layouts  2.59 us

profile of v3, /device:TPU:12, one launch (start us, length us, event | category | flops | bytes accessed | tf_op | source)
XLA Modules:
  0.0 95.3 jit_solution(16144427775925180714)
XLA Ops:
  0.0 0.0 copy-start.8
  0.0 0.8 reshape.9.counts
  0.8 0.0 copy-start
  0.8 1.0 %copy-done = f32[32,32,128]{2,1,0:T(8,128)S(1)} copy-done((f32[32,32,128]{2,1,0:T(8,128)S(1)}, f32[32,32,128]{2,1,0:T(8,128)}, u32[]{:S(2)}) %copy-start) | copy-done | bytes 524312
  1.8 0.0 copy-start.7
  1.8 0.7 copy-done.7
  2.5 0.0 copy-start.1
  2.5 0.0 copy-start.2
  2.5 0.0 copy-start.3
  2.5 0.0 copy-start.4
  2.5 0.0 copy-start.5
  2.6 0.0 copy-start.6
  2.6 27.1 %gather_windows.1 = f32[3,64,64,128]{3,2,1,0:T(8,128)S(1)} custom-call(f32[32,32,128]{2,1,0:T(8,128)S(1)} %copy-done, s32[32,32]{1,0:T(8,128)S(1)} %copy-done.7), custom_call_target="tpu_custom_call" | custom-call | tf_op jit(solution)/shard_map/gather_windows/pallas_call | solution.py:436
  29.6 0.0 copy-done.8
  29.7 0.0 copy-done.1
  29.7 0.0 copy-done.2
  29.7 0.0 copy-done.3
  29.7 0.0 copy-done.4
  29.7 0.0 copy-done.5
  29.7 0.0 copy-done.6
  29.7 24.7 %shrink.1 = (f32[2,4096,128]{2,1,0:T(8,128)S(1)}, f32[8,128]{1,0:T(8,128)S(1)}) custom-call(s32[4]{0:T(128)S(1)} %reshape.9.counts, s32[4]{0:T(128)S(1)} %copy-done.8, f32[3,4096,128]{2,1,0:T(8,128)S(1)} %bitcast.2, bf16[128,128]{1,0:T(8,128)(2,1)S(1)} %copy-done.6, bf16[128,128]{1,0:T(8,128)(2,1)S(1)} %copy-done.5, bf16[256,256]{1,0:T(8,128)(2,1)S(1)} %copy-done.2, ...), custom_call_target="tpu_custom_call" | custom-call | tf_op jit(solution)/shard_map/shrink/pallas_call | solution.py:203
  54.5 40.1 %scatter_windows.1 = f32[32,32,128]{2,1,0:T(8,128)S(1)} custom-call(f32[8,128]{1,0:T(8,128)S(1)} %get-tuple-element.7.flag, f32[2,64,64,128]{3,2,1,0:T(8,128)S(1)} %bitcast.3), custom_call_target="tpu_custom_call" | custom-call | tf_op jit(solution)/shard_map/scatter_windows/pallas_call | solution.py:582
  94.5 0.8 copy.12
Async XLA Ops:
  0.0 29.6 %copy-start.8 = (s32[4]{0:T(128)S(1)}, s32[4]{0:T(128)}, u32[]{:S(2)}) copy-start(s32[4]{0:T(128)} %levels.1) | copy-start | bytes 52
  0.8 1.0 %copy-start = (f32[32,32,128]{2,1,0:T(8,128)S(1)}, f32[32,32,128]{2,1,0:T(8,128)}, u32[]{:S(2)}) copy-start(f32[32,32,128]{2,1,0:T(8,128)} %traces.1) | copy-start | bytes 1572868
  1.8 0.7 copy-start.7
  2.5 27.1 %copy-start.1 = (bf16[256,256]{1,0:T(8,128)(2,1)S(1)}, bf16[256,256]{1,0:T(8,128)(2,1)}, u32[]{:S(2)}) copy-start(bf16[256,256]{1,0:T(8,128)(2,1)} %constant.15.clone.time_b) | copy-start | bytes 393220
  2.5 27.1 %copy-start.2 = (bf16[256,256]{1,0:T(8,128)(2,1)S(1)}, bf16[256,256]{1,0:T(8,128)(2,1)}, u32[]{:S(2)}) copy-start(bf16[256,256]{1,0:T(8,128)(2,1)} %constant.14.clone.time_f) | copy-start | bytes 393220
  2.5 27.1 %copy-start.3 = (f32[64,128]{1,0:T(8,128)S(1)}, f32[64,128]{1,0:T(8,128)}, u32[]{:S(2)}) copy-start(f32[64,128]{1,0:T(8,128)} %constant.17.clone.lines) | copy-start | bytes 98308
  2.5 27.1 %copy-start.4 = (f32[64,128]{1,0:T(8,128)S(1)}, f32[64,128]{1,0:T(8,128)}, u32[]{:S(2)}) copy-start(f32[64,128]{1,0:T(8,128)} %constant.16.clone.plane) | copy-start | bytes 98308
  2.5 27.1 %copy-start.5 = (bf16[128,128]{1,0:T(8,128)(2,1)S(1)}, bf16[128,128]{1,0:T(8,128)(2,1)}, u32[]{:S(2)}) copy-start(bf16[128,128]{1,0:T(8,128)(2,1)} %constant.13.clone.space_b) | copy-start | bytes 98308
  2.6 27.1 %copy-start.6 = (bf16[128,128]{1,0:T(8,128)(2,1)S(1)}, bf16[128,128]{1,0:T(8,128)(2,1)}, u32[]{:S(2)}) copy-start(bf16[128,128]{1,0:T(8,128)(2,1)} %constant.12.clone.space_f) | copy-start | bytes 98308

commit v4 on v3

--- a/solution.py
+++ b/solution.py
@@ -41,8 +41,7 @@
     space = cosine_table(WIN)
     for table in (space, space.T):
         high, low = halves(table)
-        upper = np.concatenate([high, high], axis=1)
-        out.append(np.concatenate([upper, np.concatenate([low, 0 * low], axis=1)], axis=0))
+        out.append(np.concatenate([high, high, low], axis=1))
     time = cosine_table(WIN_T)
     for table in (time.T, time):
         high, low = halves(table)
@@ -67,9 +66,8 @@
     for n in range(0, len(slices), 2):
         high, low = split(jnp.concatenate([slices[n], slices[n + 1]], axis=1))
         both = jnp.dot(
-            table, jnp.concatenate([high, low], axis=0), preferred_element_type=jnp.float32
+            table, jnp.concatenate([high, low, high], axis=0), preferred_element_type=jnp.float32
         )
-        both = both[:WIN] + both[WIN:]
         out += [both[:, :WIN_T], both[:, WIN_T:]]
     return out
 
@@ -285,6 +283,22 @@
             def _():
                 otherwise()
 
+    def arrive_coded(self, sent, then, otherwise=None):
+        _, axis, step = sent[0]
+        there = self.has(axis, -step)
+
+        @pl.when(there)
+        def _():
+            for copy, _, _ in sent:
+                copy.wait_recv()
+            then()
+
+        if otherwise is not None:
+
+            @pl.when(jnp.logical_not(there))
+            def _():
+                otherwise()
+
     def finish(self, sents):
         for copy, axis, step in sents:
 
@@ -315,6 +329,64 @@
         for q in range(QUARTERS):
             start = h * HALO + q * UNIT
             yield h, q, pl.ds(start, UNIT), pl.ds(h * UNIT, UNIT)
+
+
+TOP = 32767
+
+
+def encode(block, words, scale, gaps):
+    values = block.reshape(-1, 8, WIN_T)
+    if gaps:
+        gone = values == DEAD
+        values = jnp.where(gone, 0.0, values)
+    most = jnp.maximum(jnp.max(jnp.abs(values), axis=0), 1e-30)
+    codes = jnp.round(values * (TOP / most)[None]).astype(jnp.int32)
+    if gaps:
+        codes = jnp.where(gone, -TOP - 1, codes)
+    half = codes.shape[0] // 2
+    words[...] = codes[:half] * (2 * TOP + 2) + (codes[half:] + (TOP + 1))
+    scale[...] = most * (1.0 / TOP)
+
+
+def decode(words, scale, shape, gaps):
+    packed = words[...]
+    first = packed >> 16
+    second = (packed & 0xFFFF) - (TOP + 1)
+    codes = jnp.concatenate([first, second], axis=0)
+    values = codes.astype(jnp.float32) * scale[...][None]
+    if gaps:
+        values = jnp.where(codes == -TOP - 1, DEAD, values)
+    return values.reshape(shape)
+
+
+def code_shapes(core_x):
+    tiles = core_x // 8
+    large, small = HALO * tiles // 2, UNIT * tiles // 2
+    words = [(2, 2, n, 8, WIN_T) for n in (large, small, small)]
+    return [pltpu.VMEM(w, jnp.int32) for w in words] + [
+        pltpu.VMEM((2, 2, 3, 8, WIN_T), jnp.float32)
+    ]
+
+
+class Coder:
+    def __init__(self, send, words, scales, gaps):
+        self.send, self.words, self.scales, self.gaps = send, words, scales, gaps
+
+    def put(self, block, kind, side):
+        words, scale = self.words[kind], self.scales
+        encode(block, words.at[0, side], scale.at[0, side, kind], self.gaps)
+
+    def go(self, kind, side):
+        words, scale = self.words[kind], self.scales
+        step = 2 * side - 1
+        return (
+            self.send(words.at[0, side], words.at[1, side], "il", step),
+            self.send(scale.at[0, side, kind], scale.at[1, side, kind], "il", step),
+        )
+
+    def get(self, kind, side, shape):
+        words, scale = self.words[kind], self.scales
+        return decode(words.at[1, side], scale.at[1, side, kind], shape, self.gaps)
 
 
 def in_quarter(lanes, q):
@@ -333,6 +405,10 @@
     to_next,
     to_prev,
     ready,
+    words_raw,
+    words_early,
+    words_late,
+    scales,
     local_sems,
     send_sems,
     recv_sems,
@@ -346,7 +422,6 @@
     ones = jnp.ones((core_x, WIN_T), jnp.bfloat16)
     seen = jnp.dot(spread, ones, preferred_element_type=jnp.float32).reshape(mine.shape)
     mine[...] = jnp.where(seen > 0.5, traces[...], DEAD)
-    links.barrier()
     inner_x = pl.ds(HALO, core_x)
     low_i, high_i = pl.ds(0, HALO), pl.ds(HALO + core_i, HALO)
     sent = []
@@ -355,8 +430,11 @@
         sent.append(links.send(*args))
         return sent[-1]
 
-    raw_up = send(mine.at[pl.ds(core_i - HALO, HALO)], raw.at[low_i, inner_x], "il", 1)
-    raw_down = send(mine.at[pl.ds(0, HALO)], raw.at[high_i, inner_x], "il", -1)
+    coder = Coder(send, (words_raw, words_early, words_late), scales, True)
+    coder.put(mine[pl.ds(0, HALO)], 0, 0)
+    coder.put(mine[pl.ds(core_i - HALO, HALO)], 0, 1)
+    links.barrier()
+    waits = [(coder.go(0, 0), raw, 0, 0, high_i), (coder.go(0, 1), raw, 0, 1, low_i)]
 
     for h, q, span, row in pieces(core_i // HALO):
         block = mine[span]
@@ -380,12 +458,17 @@
 
     low_p, high_p = pl.ds(0, UNIT), pl.ds(UNIT + core_i // QUARTERS, UNIT)
     from_p = pl.ds(core_i // QUARTERS, UNIT)
-    waits = [(raw_up, raw, low_i), (raw_down, raw, high_i)]
-    for arrival, buffer, source in ((early_in, early, to_next), (late_in, late, to_prev)):
+    for arrival, buffer, source, kind in (
+        (early_in, early, to_next, 1),
+        (late_in, late, to_prev, 2),
+    ):
         links.arrive(arrival, blank(buffer, source))
-        up = send(buffer.at[from_p, inner_x], buffer.at[low_p, inner_x], "il", 1)
-        down = send(buffer.at[pl.ds(UNIT, UNIT), inner_x], buffer.at[high_p, inner_x], "il", -1)
-        waits += [(up, buffer, low_p), (down, buffer, high_p)]
+        coder.put(buffer[pl.ds(UNIT, UNIT), inner_x], kind, 0)
+        coder.put(buffer[from_p, inner_x], kind, 1)
+        waits += [
+            (coder.go(kind, 0), buffer, kind, 0, high_p),
+            (coder.go(kind, 1), buffer, kind, 1, low_p),
+        ]
 
     def missing(target, first, second):
         def fill():
@@ -394,8 +477,17 @@
 
         return fill
 
-    for arrival, buffer, place in waits:
-        links.arrive(arrival, missing(buffer, place, inner_x))
+    def restored(target, kind, side, first):
+        def fill():
+            shape = target.at[first, inner_x].shape
+            target[first, inner_x] = coder.get(kind, side, shape)
+
+        return fill
+
+    for arrival, buffer, kind, side, place in waits:
+        links.arrive_coded(
+            arrival, restored(buffer, kind, side, place), missing(buffer, place, inner_x)
+        )
 
     waits = []
     low_x, high_x = pl.ds(0, HALO), pl.ds(HALO + core_x, HALO)
@@ -407,13 +499,16 @@
     for arrival, buffer, place in waits:
         links.arrive(arrival, missing(buffer, pl.ds(0, buffer.shape[0]), place))
 
+    trades = []
     for h, q, span, row in pieces(WIN // HALO):
         block = raw[span]
         lanes = lane_numbers(block.shape)
         added = turned(late[row], WIN_T - HALO_T - q * HALO_T)
         ready[1, span] = jnp.where(lanes < WIN_T - HALO_T, turned(block, -HALO_T), added)
-    trade = links.partner(ready.at[1], out.at[2])
-    trade.start()
+        if q == QUARTERS - 1:
+            part = pl.ds(h * HALO, HALO)
+            trades.append(links.partner(ready.at[1, part], out.at[2, part]))
+            trades[-1].start()
     keep = [pltpu.make_async_copy(ready.at[n], out.at[n], local_sems.at[n]) for n in range(WPD)]
     keep[1].start()
     for h, q, span, row in pieces(WIN // HALO):
@@ -424,7 +519,8 @@
     keep[0].start()
     keep[0].wait()
     keep[1].wait()
-    trade.wait()
+    for trade in trades:
+        trade.wait()
     links.finish(sent)
 
 
@@ -433,13 +529,15 @@
     small = (traces.shape[0] // QUARTERS, traces.shape[1], WIN_T)
     scratch = [traces.shape, (WIN, WIN, WIN_T), packed, packed, small, small]
     scratch += [(WPD, WIN, WIN, WIN_T)]
+    codes = code_shapes(traces.shape[1])
     return pl.pallas_call(
         functools.partial(gather_kernel, sizes),
         out_shape=jax.ShapeDtypeStruct((3, WIN, WIN, WIN_T), jnp.float32),
         in_specs=[pl.BlockSpec(memory_space=pltpu.VMEM)] * 2,
         out_specs=pl.BlockSpec(memory_space=pl.ANY),
         scratch_shapes=[pltpu.VMEM(shape, jnp.float32) for shape in scratch]
-        + [pltpu.SemaphoreType.DMA((WPD,)), pltpu.SemaphoreType.DMA((15,)), pltpu.SemaphoreType.DMA((15,))],
+        + codes
+        + [pltpu.SemaphoreType.DMA((n,)) for n in (WPD, 24, 24)],
         compiler_params=pltpu.CompilerParams(
             collective_id=0, has_side_effects=True, vmem_limit_bytes=40 * 2**20
         ),
@@ -460,9 +558,10 @@
     side_raw,
     side_early,
     side_late,
-    edge_raw,
-    edge_early,
-    edge_late,
+    words_raw,
+    words_early,
+    words_late,
+    scales,
     from_time,
     local_sems,
     send_sems,
@@ -483,8 +582,10 @@
         sent.append(links.send(*args))
         return sent[-1]
 
-    trade = links.partner(results.at[1], foreign)
-    trade.start()
+    parts = [pl.ds(h * HALO, HALO) for h in range(WIN // HALO)]
+    trades = [links.partner(results.at[1, part], foreign.at[part]) for part in parts]
+    for trade in trades:
+        trade.start()
     for load in loads:
         load.wait()
     for h, q, span, row in pieces(WIN // HALO):
@@ -493,8 +594,9 @@
         raw[span] = jnp.where(lanes < WIN_T - HALO_T, turned(block, -HALO_T), 0.0)
         first = turned(block, q * HALO_T)
         early[row] = first if q == 0 else jnp.where(in_quarter(lanes, q), first, early[row])
-    trade.wait()
     for h, q, span, row in pieces(WIN // HALO):
+        if q == 0:
+            trades[h].wait()
         block = jnp.where(flag[...][None, :1, :] > 0.5, foreign[span], done[1, span])
         lanes = lane_numbers(block.shape)
         raw[span] = raw[span] + jnp.where(lanes >= HALO_T, turned(block, HALO_T), 0.0)
@@ -526,25 +628,32 @@
 
     gathered(waits)
 
+    coder = Coder(send, (words_raw, words_early, words_late), scales, False)
     waits = []
-    for buffer, edge, width in (
-        (early, edge_early, UNIT),
-        (late, edge_late, UNIT),
-        (raw, edge_raw, HALO),
-    ):
+    for buffer, kind, width in ((early, 1, UNIT), (late, 2, UNIT), (raw, 0, HALO)):
         total = buffer.shape[0]
         inner = total - 2 * width
-        down = send(buffer.at[pl.ds(0, width), inner_x], edge.at[0], "il", -1)
-        up = send(buffer.at[pl.ds(total - width, width), inner_x], edge.at[1], "il", 1)
+        coder.put(buffer[pl.ds(0, width), inner_x], kind, 0)
+        coder.put(buffer[pl.ds(total - width, width), inner_x], kind, 1)
         waits += [
-            (down, buffer, pl.ds(inner, width), inner_x, edge.at[0]),
-            (up, buffer, pl.ds(width, width), inner_x, edge.at[1]),
+            (coder.go(kind, 0), buffer, kind, 0, pl.ds(inner, width)),
+            (coder.go(kind, 1), buffer, kind, 1, pl.ds(width, width)),
         ]
-    gathered(waits[:4])
+
+    def added(target, kind, side, first):
+        def fill():
+            there = target[first, inner_x]
+            target[first, inner_x] = there + coder.get(kind, side, there.shape)
+
+        return fill
+
+    for arrival, buffer, kind, side, place in waits[:4]:
+        links.arrive_coded(arrival, added(buffer, kind, side, place))
     inner_p = pl.ds(UNIT, core_i // QUARTERS)
     back = send(early.at[inner_p, inner_x], from_time.at[0], "ta", -1)
     ahead = send(late.at[inner_p, inner_x], from_time.at[1], "ta", 1)
-    gathered(waits[4:])
+    for arrival, buffer, kind, side, place in waits[4:]:
+        links.arrive_coded(arrival, added(buffer, kind, side, place))
     out[...] = raw[pl.ds(HALO, core_i), inner_x]
     for arrival, side, shift in ((back, 0, WIN_T - HALO_T), (ahead, 1, 0)):
         links.arrive(arrival)
@@ -574,18 +683,17 @@
         (2, WIN, HALO, WIN_T),
         (2,) + small,
         (2,) + small,
-        (2, HALO, core_x, WIN_T),
-        (2, UNIT, core_x, WIN_T),
-        (2, UNIT, core_x, WIN_T),
-        (2, core_i // QUARTERS, core_x, WIN_T),
     ]
+    time_side = pltpu.VMEM((2, core_i // QUARTERS, core_x, WIN_T), jnp.float32)
+    codes = code_shapes(core_x) + [time_side]
     return pl.pallas_call(
         functools.partial(scatter_kernel, sizes),
         out_shape=jax.ShapeDtypeStruct(shape, jnp.float32),
         in_specs=[pl.BlockSpec(memory_space=pltpu.VMEM), pl.BlockSpec(memory_space=pl.ANY)],
         out_specs=pl.BlockSpec(memory_space=pltpu.VMEM),
         scratch_shapes=[pltpu.VMEM(shape, jnp.float32) for shape in scratch]
-        + [pltpu.SemaphoreType.DMA((WPD,)), pltpu.SemaphoreType.DMA((15,)), pltpu.SemaphoreType.DMA((15,))],
+        + codes
+        + [pltpu.SemaphoreType.DMA((n,)) for n in (WPD, 24, 24)],
         compiler_params=pltpu.CompilerParams(
             collective_id=1, has_side_effects=True, vmem_limit_bytes=40 * 2**20
         ),

time: 95.7 us -> 77.8 us (0.81)
  the two profiles are of different devices: /device:TPU:12 before, /device:TPU:0 now
where the time goes in v4:
time: 77.8 us; the launch traced here: 76.5 us
  Pallas kernels  73.1 us (94%)
  local copies, waits for them, and re-layouts  3.36 us (4%)
    pallas_call x1, Pallas kernels, reconstruct(): pl.pallas_call(shrink_kernel, in_specs=[smem, smem, hbm] + [vmem] * len(f...  29.1 us
    pallas_call x1, Pallas kernels, scatter_windows(): pl.pallas_call(functools.partial(scatter_kernel, sizes), out_shape=jax.Sh...  23.3 us
    pallas_call x1, Pallas kernels, gather_windows(): pl.pallas_call(functools.partial(gather_kernel, sizes), out_shape=jax.Sha...  20.6 us
    unnamed x19, local copies, waits for them, and re-layouts  2.59 us

profile of v4, /device:TPU:0, one launch (start us, length us, event | category | flops | bytes accessed | tf_op | source)
XLA Modules:
  0.0 76.5 jit_solution(11037920015322946996)
XLA Ops:
  0.0 0.0 copy-start.8
  0.0 0.8 %reshape.9.counts = s32[4]{0:T(128)S(1)} reshape(s32[1,2,2]{2,1,0:T(2,128)} %param.12) | data formatting | bytes 32 | tf_op jit(solution)/shard_map/reshape | solution.py:706
  0.8 0.0 copy-start
  0.8 1.0 %copy-done = f32[32,32,128]{2,1,0:T(8,128)S(1)} copy-done((f32[32,32,128]{2,1,0:T(8,128)S(1)}, f32[32,32,128]{2,1,0:T(8,128)}, u32[]{:S(2)}) %copy-start) | copy-done | bytes 524312
  1.8 0.0 copy-start.7
  1.8 0.7 copy-done.7
  2.5 0.0 copy-start.1
  2.5 0.0 copy-start.2
  2.5 0.0 copy-start.3
  2.5 0.0 copy-start.4
  2.5 0.0 copy-start.5
  2.6 0.0 copy-start.6
  2.6 20.6 %gather_windows.1 = f32[3,64,64,128]{3,2,1,0:T(8,128)S(1)} custom-call(f32[32,32,128]{2,1,0:T(8,128)S(1)} %copy-done, s32[32,32]{1,0:T(8,128)S(1)} %copy-done.7), custom_call_target="tpu_custom_call" | custom-call | tf_op jit(solution)/shard_map/gather_windows/pallas_call | solution.py:533
  23.2 0.0 copy-done.8
  23.2 0.0 copy-done.1
  23.2 0.0 copy-done.2
  23.2 0.0 copy-done.3
  23.2 0.0 copy-done.4
  23.2 0.0 copy-done.5
  23.3 0.0 copy-done.6
  23.3 29.1 %shrink.1 = (f32[2,4096,128]{2,1,0:T(8,128)S(1)}, f32[8,128]{1,0:T(8,128)S(1)}) custom-call(s32[4]{0:T(128)S(1)} %reshape.9.counts, s32[4]{0:T(128)S(1)} %copy-done.8, f32[3,4096,128]{2,1,0:T(8,128)S(1)} %bitcast.2, bf16[64,192]{1,0:T(8,128)(2,1)S(1)} %copy-done.6, bf16[64,192]{1,0:T(8,128)(2,1)S(1)} %copy-done.5, bf16[256,256]{1,0:T(8,128)(2,1)S(1)} %copy-done.2, ...), custom_call_target="tpu_custom_call" | custom-call | tf_op jit(solution)/shard_map/shrink/pallas_call | solution.py:201
  52.4 23.3 %scatter_windows.1 = f32[32,32,128]{2,1,0:T(8,128)S(1)} custom-call(f32[8,128]{1,0:T(8,128)S(1)} %get-tuple-element.7.flag, f32[2,64,64,128]{3,2,1,0:T(8,128)S(1)} %bitcast.3), custom_call_target="tpu_custom_call" | custom-call | tf_op jit(solution)/shard_map/scatter_windows/pallas_call | solution.py:689
  75.7 0.8 %copy.12 = f32[32,32,128]{2,1,0:T(8,128)} copy(f32[32,32,128]{2,1,0:T(8,128)S(1)} %scatter_windows.1) | data formatting | bytes 1048576
Async XLA Ops:
  0.0 23.2 %copy-start.8 = (s32[4]{0:T(128)S(1)}, s32[4]{0:T(128)}, u32[]{:S(2)}) copy-start(s32[4]{0:T(128)} %levels.1) | copy-start | bytes 52
  0.8 1.0 %copy-start = (f32[32,32,128]{2,1,0:T(8,128)S(1)}, f32[32,32,128]{2,1,0:T(8,128)}, u32[]{:S(2)}) copy-start(f32[32,32,128]{2,1,0:T(8,128)} %traces.1) | copy-start | bytes 1572868
  1.8 0.7 copy-start.7
  2.5 20.7 %copy-start.1 = (bf16[256,256]{1,0:T(8,128)(2,1)S(1)}, bf16[256,256]{1,0:T(8,128)(2,1)}, u32[]{:S(2)}) copy-start(bf16[256,256]{1,0:T(8,128)(2,1)} %constant.15.clone.time_b) | copy-start | bytes 393220
  2.5 20.7 %copy-start.2 = (bf16[256,256]{1,0:T(8,128)(2,1)S(1)}, bf16[256,256]{1,0:T(8,128)(2,1)}, u32[]{:S(2)}) copy-start(bf16[256,256]{1,0:T(8,128)(2,1)} %constant.14.clone.time_f) | copy-start | bytes 393220
  2.5 20.7 %copy-start.3 = (f32[64,128]{1,0:T(8,128)S(1)}, f32[64,128]{1,0:T(8,128)}, u32[]{:S(2)}) copy-start(f32[64,128]{1,0:T(8,128)} %constant.17.clone.lines) | copy-start | bytes 98308
  2.5 20.7 %copy-start.4 = (f32[64,128]{1,0:T(8,128)S(1)}, f32[64,128]{1,0:T(8,128)}, u32[]{:S(2)}) copy-start(f32[64,128]{1,0:T(8,128)} %constant.16.clone.plane) | copy-start | bytes 98308
  2.5 20.7 %copy-start.5 = (bf16[64,192]{1,0:T(8,128)(2,1)S(1)}, bf16[64,192]{1,0:T(8,128)(2,1)}, u32[]{:S(2)}) copy-start(bf16[64,192]{1,0:T(8,128)(2,1)} %constant.13.clone.space_b) | copy-start | bytes 73732
  2.6 20.7 %copy-start.6 = (bf16[64,192]{1,0:T(8,128)(2,1)S(1)}, bf16[64,192]{1,0:T(8,128)(2,1)}, u32[]{:S(2)}) copy-start(bf16[64,192]{1,0:T(8,128)(2,1)} %constant.12.clone.space_f) | copy-start | bytes 73732

commit v5 on v4

--- a/solution.py
+++ b/solution.py
@@ -15,7 +15,9 @@
 HALO_T = 32
 DEAD = 1e30
 PITCH = 72
-GROUP = 16
+GROUP = 32
+CHUNK = GROUP * WIN
+CHUNKS = WIN // GROUP
 
 
 def cosine_table(order):
@@ -101,31 +103,65 @@
 ):
     me = lax.axis_index("xl")
     other = me + 1 - 2 * lax.rem(me, 2)
-    own_first, own_final = counts[WPD * me], counts[WPD * me + 1]
-    other_first, other_final = counts[WPD * other], counts[WPD * other + 1]
+    own_first, own_final = counts[0, me, 0], counts[0, me, WPD - 1]
+    other_first, other_final = counts[0, other, 0], counts[0, other, WPD - 1]
     before = jnp.maximum(own_first + own_final, other_first + other_final)
     after = jnp.maximum(own_first + other_final, other_first + own_final)
     trading = after < before
     flag[...] = jnp.full(flag.shape, jnp.where(trading, 1.0, 0.0), jnp.float32)
     second = jnp.where(trading, 2, 1)
-    pltpu.make_async_copy(windows.at[0], window.at[0], in_sems.at[0]).start()
-    pltpu.make_async_copy(windows.at[second], window.at[1], in_sems.at[1]).start()
+
+    def load(slot, source, chunk):
+        rows = pl.ds(chunk * CHUNK, CHUNK)
+        return pltpu.make_async_copy(
+            windows.at[source, rows], window.at[slot, rows], in_sems.at[slot, chunk]
+        )
+
+    def store(slot, chunk):
+        rows = pl.ds(chunk * CHUNK, CHUNK)
+        return pltpu.make_async_copy(
+            ready.at[slot, rows], out.at[slot, rows], out_sems.at[slot, chunk]
+        )
+
+    for slot, source in enumerate((0, second)):
+        for chunk in range(CHUNKS):
+            load(slot, source, chunk).start()
 
     @pl.loop(0, WPD)
     def _(slot):
-        pltpu.make_async_copy(windows.at[slot], window.at[slot], in_sems.at[slot]).wait()
         final = jnp.where(trading, other_final, own_final)
         count = jnp.where(slot == 0, own_first, final)
         tables = (space_f, space_b, time_f, time_b, plane, lines)
-        shrink_window(count, levels, window.at[slot], *tables, ready.at[slot], held)
-        pltpu.make_async_copy(ready.at[slot], out.at[slot], out_sems.at[slot]).start()
+        shrink_window(
+            count,
+            levels,
+            window.at[slot],
+            *tables,
+            ready.at[slot],
+            held,
+            lambda group: load(slot, slot, group).wait(),
+            lambda group: store(slot, group).start(),
+        )
 
     for slot in range(WPD):
-        pltpu.make_async_copy(ready.at[slot], out.at[slot], out_sems.at[slot]).wait()
+        for chunk in range(CHUNKS):
+            store(slot, chunk).wait()
 
 
 def shrink_window(
-    count, levels, window, space_f, space_b, time_f, time_b, plane, lines, out, held
+    count,
+    levels,
+    window,
+    space_f,
+    space_b,
+    time_f,
+    time_b,
+    plane,
+    lines,
+    out,
+    held,
+    take,
+    give,
 ):
     last = count - 1
 
@@ -153,6 +189,7 @@
 
     @pl.loop(0, WIN // GROUP)
     def _(group):
+        take(group)
         estimates = []
         for n in range(GROUP):
             known = recorded(group, n)
@@ -190,6 +227,7 @@
             start = pl.multiple_of(line * WIN, 8)
             weight = lines[pl.ds(line, 1), :]
             out[pl.ds(start, WIN), :] = estimates[n] * (plane[...] * weight)
+        give(group)
 
 
 def reconstruct(windows, counts, levels):
@@ -210,8 +248,8 @@
             pltpu.VMEM((WIN * PITCH, WIN_T), jnp.float32),
             pltpu.VMEM(shape, jnp.float32),
             pltpu.VMEM(shape, jnp.float32),
-            pltpu.SemaphoreType.DMA((WPD,)),
-            pltpu.SemaphoreType.DMA((WPD,)),
+            pltpu.SemaphoreType.DMA((WPD, CHUNKS)),
+            pltpu.SemaphoreType.DMA((WPD, CHUNKS)),
         ],
         compiler_params=pltpu.CompilerParams(vmem_limit_bytes=40 * 2**20),
         name="shrink",
@@ -229,7 +267,7 @@
             return self.me[axis] < self.sizes[axis] - 1
         return self.me[axis] > 0
 
-    def barrier(self):
+    def greet(self):
         barrier = pltpu.get_barrier_semaphore()
         total = 0
         for axis in self.sizes:
@@ -246,6 +284,10 @@
                         device_id_type=pl.DeviceIdType.MESH,
                     )
 
+        return barrier, total
+
+    def barrier(self):
+        barrier, total = self.greet()
         pl.semaphore_wait(barrier, total)
 
     def copy(self, source, target, axis, index):
@@ -415,13 +457,17 @@
 ):
     links = Links(sizes, send_sems, recv_sems)
     core_i, core_x, _ = mine.shape
+    own = pltpu.make_async_copy(traces, mine, local_sems.at[0])
+    own.start()
+    barrier, total = links.greet()
     square = (core_x, core_x)
     same = lax.broadcasted_iota(jnp.int32, square, 0) == lax.broadcasted_iota(jnp.int32, square, 1)
     spread = [jnp.where(same, live[pl.ds(n, 1), :], 0) for n in range(core_i)]
     spread = jnp.concatenate(spread, axis=0).astype(jnp.float32).astype(jnp.bfloat16)
     ones = jnp.ones((core_x, WIN_T), jnp.bfloat16)
     seen = jnp.dot(spread, ones, preferred_element_type=jnp.float32).reshape(mine.shape)
-    mine[...] = jnp.where(seen > 0.5, traces[...], DEAD)
+    own.wait()
+    mine[...] = jnp.where(seen > 0.5, mine[...], DEAD)
     inner_x = pl.ds(HALO, core_x)
     low_i, high_i = pl.ds(0, HALO), pl.ds(HALO + core_i, HALO)
     sent = []
@@ -433,7 +479,7 @@
     coder = Coder(send, (words_raw, words_early, words_late), scales, True)
     coder.put(mine[pl.ds(0, HALO)], 0, 0)
     coder.put(mine[pl.ds(core_i - HALO, HALO)], 0, 1)
-    links.barrier()
+    pl.semaphore_wait(barrier, total)
     waits = [(coder.go(0, 0), raw, 0, 0, high_i), (coder.go(0, 1), raw, 0, 1, low_i)]
 
     for h, q, span, row in pieces(core_i // HALO):
@@ -533,7 +579,10 @@
     return pl.pallas_call(
         functools.partial(gather_kernel, sizes),
         out_shape=jax.ShapeDtypeStruct((3, WIN, WIN, WIN_T), jnp.float32),
-        in_specs=[pl.BlockSpec(memory_space=pltpu.VMEM)] * 2,
+        in_specs=[
+            pl.BlockSpec(memory_space=pl.ANY),
+            pl.BlockSpec(memory_space=pltpu.VMEM),
+        ],
         out_specs=pl.BlockSpec(memory_space=pl.ANY),
         scratch_shapes=[pltpu.VMEM(shape, jnp.float32) for shape in scratch]
         + codes
@@ -703,7 +752,7 @@
 
 def shards(sizes, traces, live, counts, levels):
     windows = gather_windows(traces, live, sizes).reshape(3, WIN * WIN, WIN_T)
-    done, flag = reconstruct(windows, counts.reshape(-1), levels)
+    done, flag = reconstruct(windows, counts, levels)
     return scatter_windows(flag, done.reshape(WPD, WIN, WIN, WIN_T), traces.shape, sizes)
 
 

time: 77.8 us -> 70.3 us (0.904)
  Pallas kernels: 73.1 us -> 66.6 us
    pallas_call x1, Pallas kernels: 23.3 us -> 18.5 us  [scatter_windows(): pl.pallas_call(functools.partial(scatter_kernel, sizes), out_shape=jax.Sh...]
    pallas_call x1, Pallas kernels: 29.1 us -> 27.7 us  [reconstruct(): pl.pallas_call(shrink_kernel, in_specs=[smem, smem, hbm] + [vmem] * len(f...]
    unnamed x19 -> x21, local copies, waits for them, and re-layouts: 2.59 us -> 2.59 us
where the time goes in v5:
time: 70.3 us; the launch traced here: 69.3 us
  Pallas kernels  66.6 us (95%)
  local copies, waits for them, and re-layouts  2.59 us (4%)
    pallas_call x1, Pallas kernels, reconstruct(): pl.pallas_call(shrink_kernel, in_specs=[smem, smem, hbm] + [vmem] * len(f...  27.7 us
    pallas_call x1, Pallas kernels, gather_windows(): pl.pallas_call(functools.partial(gather_kernel, sizes), out_shape=jax.Sha...  20.3 us
    pallas_call x1, Pallas kernels, scatter_windows(): pl.pallas_call(functools.partial(scatter_kernel, sizes), out_shape=jax.Sh...  18.5 us
    unnamed x21, local copies, waits for them, and re-layouts  2.59 us

profile of v5, /device:TPU:0, one launch (start us, length us, event | category | flops | bytes accessed | tf_op | source)
XLA Modules:
  0.0 69.3 jit_solution(18158756326495295261)
XLA Ops:
  0.0 0.0 copy-start
  0.0 1.0 %copy-done = f32[32,32,128]{2,1,0:T(8,128)S(1)} copy-done((f32[32,32,128]{2,1,0:T(8,128)S(1)}, f32[32,32,128]{2,1,0:T(8,128)}, u32[]{:S(2)}) %copy-start) | copy-done | bytes 524312
  1.0 0.0 copy-start.7
  1.0 0.7 %copy-done.7 = s32[32,32]{1,0:T(8,128)S(1)} copy-done((s32[32,32]{1,0:T(8,128)S(1)}, s32[32,32]{1,0:T(8,128)}, u32[]{:S(2)}) %copy-start.7) | copy-done | bytes 4120
  1.8 0.0 copy-start.1
  1.8 0.0 copy-start.2
  1.8 0.0 copy-start.3
  1.8 0.0 copy-start.4
  1.8 0.0 copy-start.5
  1.8 0.0 copy-start.6
  1.8 0.0 copy-start.8
  1.8 0.0 copy-start.9
  1.8 20.3 %gather_windows.1 = f32[3,64,64,128]{3,2,1,0:T(8,128)S(1)} custom-call(f32[32,32,128]{2,1,0:T(8,128)S(1)} %copy-done, s32[32,32]{1,0:T(8,128)S(1)} %copy-done.7), custom_call_target="tpu_custom_call" | custom-call | tf_op jit(solution)/shard_map/gather_windows/pallas_call | solution.py:579
  22.1 0.0 copy-done.1
  22.2 0.0 copy-done.2
  22.2 0.0 copy-done.3
  22.2 0.0 copy-done.4
  22.2 0.0 copy-done.5
  22.2 0.0 copy-done.6
  22.2 0.0 copy-done.8
  22.2 0.0 copy-done.9
  22.2 27.7 %shrink.1 = (f32[2,4096,128]{2,1,0:T(8,128)S(1)}, f32[8,128]{1,0:T(8,128)S(1)}) custom-call(s32[1,2,2]{2,1,0:T(2,128)S(1)} %copy-done.8, s32[4]{0:T(128)S(1)} %copy-done.9, f32[3,4096,128]{2,1,0:T(8,128)S(1)} %bitcast.2, bf16[64,192]{1,0:T(8,128)(2,1)S(1)} %copy-done.6, bf16[64,192]{1,0:T(8,128)(2,1)S(1)} %copy-done.5, bf16[256,256]{1,0:T(8,128)(2,1)S(1)} %copy-done.2, ...), custom_call_target="tpu_custom_call" | custom-call | tf_op jit(solution)/shard_map/shrink/pallas_call | solution.py:239
  50.0 18.5 %scatter_windows.1 = f32[32,32,128]{2,1,0:T(8,128)S(1)} custom-call(f32[8,128]{1,0:T(8,128)S(1)} %get-tuple-element.7.flag, f32[2,64,64,128]{3,2,1,0:T(8,128)S(1)} %bitcast.3), custom_call_target="tpu_custom_call" | custom-call | tf_op jit(solution)/shard_map/scatter_windows/pallas_call | solution.py:738
  68.5 0.8 %copy.12 = f32[32,32,128]{2,1,0:T(8,128)} copy(f32[32,32,128]{2,1,0:T(8,128)S(1)} %scatter_windows.1) | data formatting | bytes 1048576
Async XLA Ops:
  0.0 1.0 %copy-start = (f32[32,32,128]{2,1,0:T(8,128)S(1)}, f32[32,32,128]{2,1,0:T(8,128)}, u32[]{:S(2)}) copy-start(f32[32,32,128]{2,1,0:T(8,128)} %traces.1) | copy-start | bytes 1572868
  1.0 0.7 %copy-start.7 = (s32[32,32]{1,0:T(8,128)S(1)}, s32[32,32]{1,0:T(8,128)}, u32[]{:S(2)}) copy-start(s32[32,32]{1,0:T(8,128)} %live.1) | copy-start | bytes 12292
  1.8 20.4 %copy-start.1 = (bf16[256,256]{1,0:T(8,128)(2,1)S(1)}, bf16[256,256]{1,0:T(8,128)(2,1)}, u32[]{:S(2)}) copy-start(bf16[256,256]{1,0:T(8,128)(2,1)} %constant.15.clone.time_b) | copy-start | bytes 393220
  1.8 20.4 %copy-start.2 = (bf16[256,256]{1,0:T(8,128)(2,1)S(1)}, bf16[256,256]{1,0:T(8,128)(2,1)}, u32[]{:S(2)}) copy-start(bf16[256,256]{1,0:T(8,128)(2,1)} %constant.14.clone.time_f) | copy-start | bytes 393220
  1.8 20.4 %copy-start.3 = (f32[64,128]{1,0:T(8,128)S(1)}, f32[64,128]{1,0:T(8,128)}, u32[]{:S(2)}) copy-start(f32[64,128]{1,0:T(8,128)} %constant.17.clone.lines) | copy-start | bytes 98308
  1.8 20.4 %copy-start.4 = (f32[64,128]{1,0:T(8,128)S(1)}, f32[64,128]{1,0:T(8,128)}, u32[]{:S(2)}) copy-start(f32[64,128]{1,0:T(8,128)} %constant.16.clone.plane) | copy-start | bytes 98308
  1.8 20.4 %copy-start.5 = (bf16[64,192]{1,0:T(8,128)(2,1)S(1)}, bf16[64,192]{1,0:T(8,128)(2,1)}, u32[]{:S(2)}) copy-start(bf16[64,192]{1,0:T(8,128)(2,1)} %constant.13.clone.space_b) | copy-start | bytes 73732
  1.8 20.4 %copy-start.6 = (bf16[64,192]{1,0:T(8,128)(2,1)S(1)}, bf16[64,192]{1,0:T(8,128)(2,1)}, u32[]{:S(2)}) copy-start(bf16[64,192]{1,0:T(8,128)(2,1)} %constant.12.clone.space_f) | copy-start | bytes 73732
  1.8 20.4 %copy-start.8 = (s32[1,2,2]{2,1,0:T(2,128)S(1)}, s32[1,2,2]{2,1,0:T(2,128)}, u32[]{:S(2)}) copy-start(s32[1,2,2]{2,1,0:T(2,128)} %counts.1) | copy-start | bytes 52
  1.8 20.4 %copy-start.9 = (s32[4]{0:T(128)S(1)}, s32[4]{0:T(128)}, u32[]{:S(2)}) copy-start(s32[4]{0:T(128)} %levels.1) | copy-start | bytes 52

commit v6 on v5

--- a/solution.py
+++ b/solution.py
@@ -15,9 +15,10 @@
 HALO_T = 32
 DEAD = 1e30
 PITCH = 72
-GROUP = 32
-CHUNK = GROUP * WIN
-CHUNKS = WIN // GROUP
+GROUP = 64
+PIECE = 16
+CHUNK = PIECE * WIN
+CHUNKS = WIN // PIECE
 
 
 def cosine_table(order):
@@ -139,8 +140,8 @@
             *tables,
             ready.at[slot],
             held,
-            lambda group: load(slot, slot, group).wait(),
-            lambda group: store(slot, group).start(),
+            lambda chunk: load(slot, slot, chunk).wait(),
+            lambda chunk: store(slot, chunk).start(),
         )
 
     for slot in range(WPD):
@@ -189,9 +190,10 @@
 
     @pl.loop(0, WIN // GROUP)
     def _(group):
-        take(group)
         estimates = []
         for n in range(GROUP):
+            if n % PIECE == 0:
+                take(group * (GROUP // PIECE) + n // PIECE)
             known = recorded(group, n)
             estimates.append(jnp.where(known == DEAD, 0.0, known))
         forward(group, estimates)
@@ -227,7 +229,8 @@
             start = pl.multiple_of(line * WIN, 8)
             weight = lines[pl.ds(line, 1), :]
             out[pl.ds(start, WIN), :] = estimates[n] * (plane[...] * weight)
-        give(group)
+            if n % PIECE == PIECE - 1:
+                give(group * (GROUP // PIECE) + n // PIECE)
 
 
 def reconstruct(windows, counts, levels):
@@ -438,9 +441,10 @@
 def gather_kernel(
     sizes,
     traces,
-    live,
+    flags,
     out,
     mine,
+    live,
     raw,
     early,
     late,
@@ -459,7 +463,10 @@
     core_i, core_x, _ = mine.shape
     own = pltpu.make_async_copy(traces, mine, local_sems.at[0])
     own.start()
+    known = pltpu.make_async_copy(flags, live, local_sems.at[1])
+    known.start()
     barrier, total = links.greet()
+    known.wait()
     square = (core_x, core_x)
     same = lax.broadcasted_iota(jnp.int32, square, 0) == lax.broadcasted_iota(jnp.int32, square, 1)
     spread = [jnp.where(same, live[pl.ds(n, 1), :], 0) for n in range(core_i)]
@@ -580,11 +587,12 @@
         functools.partial(gather_kernel, sizes),
         out_shape=jax.ShapeDtypeStruct((3, WIN, WIN, WIN_T), jnp.float32),
         in_specs=[
-            pl.BlockSpec(memory_space=pl.ANY),
-            pl.BlockSpec(memory_space=pltpu.VMEM),
+            pl.BlockSpec(memory_space=pltpu.HBM),
+            pl.BlockSpec(memory_space=pltpu.HBM),
         ],
         out_specs=pl.BlockSpec(memory_space=pl.ANY),
-        scratch_shapes=[pltpu.VMEM(shape, jnp.float32) for shape in scratch]
+        scratch_shapes=[pltpu.VMEM(traces.shape, jnp.float32), pltpu.VMEM(live.shape, jnp.int32)]
+        + [pltpu.VMEM(shape, jnp.float32) for shape in scratch[1:]]
         + codes
         + [pltpu.SemaphoreType.DMA((n,)) for n in (WPD, 24, 24)],
         compiler_params=pltpu.CompilerParams(

time: 70.3 us -> 68.9 us (0.980)
  Pallas kernels: 66.6 us -> 64.9 us
    pallas_call x1, Pallas kernels: 27.7 us -> 26.4 us  [reconstruct(): pl.pallas_call(shrink_kernel, in_specs=[smem, smem, hbm] + [vmem] * len(f...]
where the time goes in v6:
time: 68.9 us; the launch traced here: 67.6 us
  Pallas kernels  64.9 us (94%)
  local copies, waits for them, and re-layouts  2.59 us (4%)
    pallas_call x1, Pallas kernels, reconstruct(): pl.pallas_call(shrink_kernel, in_specs=[smem, smem, hbm] + [vmem] * len(f...  26.4 us
    pallas_call x1, Pallas kernels, gather_windows(): pl.pallas_call(functools.partial(gather_kernel, sizes), out_shape=jax.Sha...  20.3 us
    pallas_call x1, Pallas kernels, scatter_windows(): pl.pallas_call(functools.partial(scatter_kernel, sizes), out_shape=jax.Sh...  18.1 us
    unnamed x21, local copies, waits for them, and re-layouts  2.59 us

profile of v6, /device:TPU:0, one launch (start us, length us, event | category | flops | bytes accessed | tf_op | source)
XLA Modules:
  0.0 67.6 jit_solution(12985649903460098098)
XLA Ops:
  0.0 0.0 copy-start
  0.0 1.0 %copy-done = f32[32,32,128]{2,1,0:T(8,128)S(1)} copy-done((f32[32,32,128]{2,1,0:T(8,128)S(1)}, f32[32,32,128]{2,1,0:T(8,128)}, u32[]{:S(2)}) %copy-start) | copy-done | bytes 524312
  1.0 0.0 copy-start.7
  1.0 0.7 %copy-done.7 = s32[32,32]{1,0:T(8,128)S(1)} copy-done((s32[32,32]{1,0:T(8,128)S(1)}, s32[32,32]{1,0:T(8,128)}, u32[]{:S(2)}) %copy-start.7) | copy-done | bytes 4120
  1.8 0.0 copy-start.1
  1.8 0.0 copy-start.2
  1.8 0.0 copy-start.3
  1.8 0.0 copy-start.4
  1.8 0.0 copy-start.5
  1.8 0.0 copy-start.6
  1.8 0.0 copy-start.8
  1.8 0.0 copy-start.9
  1.8 20.3 %gather_windows.1 = f32[3,64,64,128]{3,2,1,0:T(8,128)S(1)} custom-call(f32[32,32,128]{2,1,0:T(8,128)S(1)} %copy-done, s32[32,32]{1,0:T(8,128)S(1)} %copy-done.7), custom_call_target="tpu_custom_call" | custom-call | tf_op jit(solution)/shard_map/gather_windows/pallas_call | solution.py:586
  22.2 0.0 copy-done.1
  22.2 0.0 copy-done.2
  22.2 0.0 copy-done.3
  22.2 0.0 copy-done.4
  22.2 0.0 copy-done.5
  22.2 0.0 copy-done.6
  22.2 0.0 copy-done.8
  22.2 0.0 copy-done.9
  22.2 26.4 %shrink.1 = (f32[2,4096,128]{2,1,0:T(8,128)S(1)}, f32[8,128]{1,0:T(8,128)S(1)}) custom-call(s32[1,2,2]{2,1,0:T(2,128)S(1)} %copy-done.8, s32[4]{0:T(128)S(1)} %copy-done.9, f32[3,4096,128]{2,1,0:T(8,128)S(1)} %bitcast.2, bf16[64,192]{1,0:T(8,128)(2,1)S(1)} %copy-done.6, bf16[64,192]{1,0:T(8,128)(2,1)S(1)} %copy-done.5, bf16[256,256]{1,0:T(8,128)(2,1)S(1)} %copy-done.2, ...), custom_call_target="tpu_custom_call" | custom-call | tf_op jit(solution)/shard_map/shrink/pallas_call | solution.py:242
  48.7 18.1 %scatter_windows.1 = f32[32,32,128]{2,1,0:T(8,128)S(1)} custom-call(f32[8,128]{1,0:T(8,128)S(1)} %get-tuple-element.7.flag, f32[2,64,64,128]{3,2,1,0:T(8,128)S(1)} %bitcast.3), custom_call_target="tpu_custom_call" | custom-call | tf_op jit(solution)/shard_map/scatter_windows/pallas_call | solution.py:746
  66.8 0.8 %copy.12 = f32[32,32,128]{2,1,0:T(8,128)} copy(f32[32,32,128]{2,1,0:T(8,128)S(1)} %scatter_windows.1) | data formatting | bytes 1048576
Async XLA Ops:
  0.0 1.0 %copy-start = (f32[32,32,128]{2,1,0:T(8,128)S(1)}, f32[32,32,128]{2,1,0:T(8,128)}, u32[]{:S(2)}) copy-start(f32[32,32,128]{2,1,0:T(8,128)} %traces.1) | copy-start | bytes 1572868
  1.0 0.7 %copy-start.7 = (s32[32,32]{1,0:T(8,128)S(1)}, s32[32,32]{1,0:T(8,128)}, u32[]{:S(2)}) copy-start(s32[32,32]{1,0:T(8,128)} %flags.1) | copy-start | bytes 12292
  1.8 20.4 %copy-start.1 = (bf16[256,256]{1,0:T(8,128)(2,1)S(1)}, bf16[256,256]{1,0:T(8,128)(2,1)}, u32[]{:S(2)}) copy-start(bf16[256,256]{1,0:T(8,128)(2,1)} %constant.15.clone.time_b) | copy-start | bytes 393220
  1.8 20.4 %copy-start.2 = (bf16[256,256]{1,0:T(8,128)(2,1)S(1)}, bf16[256,256]{1,0:T(8,128)(2,1)}, u32[]{:S(2)}) copy-start(bf16[256,256]{1,0:T(8,128)(2,1)} %constant.14.clone.time_f) | copy-start | bytes 393220
  1.8 20.4 %copy-start.3 = (f32[64,128]{1,0:T(8,128)S(1)}, f32[64,128]{1,0:T(8,128)}, u32[]{:S(2)}) copy-start(f32[64,128]{1,0:T(8,128)} %constant.17.clone.lines) | copy-start | bytes 98308
  1.8 20.4 %copy-start.4 = (f32[64,128]{1,0:T(8,128)S(1)}, f32[64,128]{1,0:T(8,128)}, u32[]{:S(2)}) copy-start(f32[64,128]{1,0:T(8,128)} %constant.16.clone.plane) | copy-start | bytes 98308
  1.8 20.4 %copy-start.5 = (bf16[64,192]{1,0:T(8,128)(2,1)S(1)}, bf16[64,192]{1,0:T(8,128)(2,1)}, u32[]{:S(2)}) copy-start(bf16[64,192]{1,0:T(8,128)(2,1)} %constant.13.clone.space_b) | copy-start | bytes 73732
  1.8 20.4 %copy-start.6 = (bf16[64,192]{1,0:T(8,128)(2,1)S(1)}, bf16[64,192]{1,0:T(8,128)(2,1)}, u32[]{:S(2)}) copy-start(bf16[64,192]{1,0:T(8,128)(2,1)} %constant.12.clone.space_f) | copy-start | bytes 73732
  1.8 20.4 %copy-start.8 = (s32[1,2,2]{2,1,0:T(2,128)S(1)}, s32[1,2,2]{2,1,0:T(2,128)}, u32[]{:S(2)}) copy-start(s32[1,2,2]{2,1,0:T(2,128)} %counts.1) | copy-start | bytes 52
  1.8 20.4 %copy-start.9 = (s32[4]{0:T(128)S(1)}, s32[4]{0:T(128)}, u32[]{:S(2)}) copy-start(s32[4]{0:T(128)} %levels.1) | copy-start | bytes 52

commit v7 on v6

--- a/solution.py
+++ b/solution.py
@@ -549,19 +549,30 @@
         up = send(buffer.at[whole, pl.ds(core_x, HALO)], buffer.at[whole, low_x], "xl", 1)
         down = send(buffer.at[whole, pl.ds(HALO, HALO)], buffer.at[whole, high_x], "xl", -1)
         waits += [(up, buffer, low_x), (down, buffer, high_x)]
+
+    def final_window(span, row, columns):
+        block = raw[span, columns]
+        lanes = lane_numbers(block.shape)
+        shift = WIN_T - HALO_T - q * HALO_T
+        added = turned(late[row, columns], shift)
+        whole = jnp.where(lanes < WIN_T - HALO_T, turned(block, -HALO_T), added)
+        ready[1, span, columns] = whole
+
+    trades = []
+    for h, q, span, row in pieces(WIN // HALO):
+        final_window(span, row, inner_x)
+        if q == QUARTERS - 1:
+            part = pl.ds(h * HALO, HALO)
+            trades.append(links.partner(ready.at[1, part, inner_x], out.at[2, part, inner_x]))
+            trades[-1].start()
     for arrival, buffer, place in waits:
         links.arrive(arrival, missing(buffer, pl.ds(0, buffer.shape[0]), place))
-
-    trades = []
-    for h, q, span, row in pieces(WIN // HALO):
-        block = raw[span]
-        lanes = lane_numbers(block.shape)
-        added = turned(late[row], WIN_T - HALO_T - q * HALO_T)
-        ready[1, span] = jnp.where(lanes < WIN_T - HALO_T, turned(block, -HALO_T), added)
-        if q == QUARTERS - 1:
-            part = pl.ds(h * HALO, HALO)
-            trades.append(links.partner(ready.at[1, part], out.at[2, part]))
-            trades[-1].start()
+    for columns in (low_x, high_x):
+        for h, q, span, row in pieces(WIN // HALO):
+            final_window(span, row, columns)
+        trades.append(links.partner(ready.at[1, :, columns], out.at[2, :, columns]))
+        trades[-1].start()
+
     keep = [pltpu.make_async_copy(ready.at[n], out.at[n], local_sems.at[n]) for n in range(WPD)]
     keep[1].start()
     for h, q, span, row in pieces(WIN // HALO):
@@ -594,7 +605,7 @@
         scratch_shapes=[pltpu.VMEM(traces.shape, jnp.float32), pltpu.VMEM(live.shape, jnp.int32)]
         + [pltpu.VMEM(shape, jnp.float32) for shape in scratch[1:]]
         + codes
-        + [pltpu.SemaphoreType.DMA((n,)) for n in (WPD, 24, 24)],
+        + [pltpu.SemaphoreType.DMA((n,)) for n in (WPD, 28, 28)],
         compiler_params=pltpu.CompilerParams(
             collective_id=0, has_side_effects=True, vmem_limit_bytes=40 * 2**20
         ),
@@ -750,7 +761,7 @@
         out_specs=pl.BlockSpec(memory_space=pltpu.VMEM),
         scratch_shapes=[pltpu.VMEM(shape, jnp.float32) for shape in scratch]
         + codes
-        + [pltpu.SemaphoreType.DMA((n,)) for n in (WPD, 24, 24)],
+        + [pltpu.SemaphoreType.DMA((n,)) for n in (WPD, 28, 28)],
         compiler_params=pltpu.CompilerParams(
             collective_id=1, has_side_effects=True, vmem_limit_bytes=40 * 2**20
         ),

time: 68.9 us -> 67.7 us (0.983); the launches traced: 67.6 us -> 67.2 us
    pallas_call x1, Pallas kernels: 18.1 us -> 22.9 us  [scatter_windows(): pl.pallas_call(functools.partial(scatter_kernel, sizes), out_shape=jax.Sh...]
    pallas_call x1, Pallas kernels: 26.4 us -> 22.5 us  [reconstruct(): pl.pallas_call(shrink_kernel, in_specs=[smem, smem, hbm] + [vmem] * len(f...]
    pallas_call x1, Pallas kernels: 20.3 us -> 19.1 us  [gather_windows(): pl.pallas_call(functools.partial(gather_kernel, sizes), out_shape=jax.Sha...]
where the time goes in v7:
time: 67.7 us; the launch traced here: 67.2 us
  Pallas kernels  64.5 us (95%)
  local copies, waits for them, and re-layouts  2.59 us (4%)
    pallas_call x1, Pallas kernels, scatter_windows(): pl.pallas_call(functools.partial(scatter_kernel, sizes), out_shape=jax.Sh...  22.9 us
    pallas_call x1, Pallas kernels, reconstruct(): pl.pallas_call(shrink_kernel, in_specs=[smem, smem, hbm] + [vmem] * len(f...  22.5 us
    pallas_call x1, Pallas kernels, gather_windows(): pl.pallas_call(functools.partial(gather_kernel, sizes), out_shape=jax.Sha...  19.1 us
    unnamed x21, local copies, waits for them, and re-layouts  2.59 us

profile of v7, /device:TPU:0, one launch (start us, length us, event | category | flops | bytes accessed | tf_op | source)
XLA Modules:
  0.0 67.2 jit_solution(9374131117324882572)
XLA Ops:
  0.0 0.0 copy-start
  0.0 1.0 %copy-done = f32[32,32,128]{2,1,0:T(8,128)S(1)} copy-done((f32[32,32,128]{2,1,0:T(8,128)S(1)}, f32[32,32,128]{2,1,0:T(8,128)}, u32[]{:S(2)}) %copy-start) | copy-done | bytes 524312
  1.0 0.0 copy-start.7
  1.0 0.7 %copy-done.7 = s32[32,32]{1,0:T(8,128)S(1)} copy-done((s32[32,32]{1,0:T(8,128)S(1)}, s32[32,32]{1,0:T(8,128)}, u32[]{:S(2)}) %copy-start.7) | copy-done | bytes 4120
  1.8 0.0 copy-start.1
  1.8 0.0 copy-start.2
  1.8 0.0 copy-start.3
  1.8 0.0 copy-start.4
  1.8 0.0 copy-start.5
  1.8 0.0 copy-start.6
  1.8 0.0 copy-start.8
  1.8 0.0 copy-start.9
  1.8 19.1 %gather_windows.1 = f32[3,64,64,128]{3,2,1,0:T(8,128)S(1)} custom-call(f32[32,32,128]{2,1,0:T(8,128)S(1)} %copy-done, s32[32,32]{1,0:T(8,128)S(1)} %copy-done.7), custom_call_target="tpu_custom_call" | custom-call | tf_op jit(solution)/shard_map/gather_windows/pallas_call | solution.py:597
  20.9 0.0 copy-done.1
  20.9 0.0 copy-done.2
  20.9 0.0 copy-done.3
  20.9 0.0 copy-done.4
  20.9 0.0 copy-done.5
  21.0 0.0 copy-done.6
  21.0 0.0 copy-done.8
  21.0 0.0 copy-done.9
  21.0 22.5 %shrink.1 = (f32[2,4096,128]{2,1,0:T(8,128)S(1)}, f32[8,128]{1,0:T(8,128)S(1)}) custom-call(s32[1,2,2]{2,1,0:T(2,128)S(1)} %copy-done.8, s32[4]{0:T(128)S(1)} %copy-done.9, f32[3,4096,128]{2,1,0:T(8,128)S(1)} %bitcast.2, bf16[64,192]{1,0:T(8,128)(2,1)S(1)} %copy-done.6, bf16[64,192]{1,0:T(8,128)(2,1)S(1)} %copy-done.5, bf16[256,256]{1,0:T(8,128)(2,1)S(1)} %copy-done.2, ...), custom_call_target="tpu_custom_call" | custom-call | tf_op jit(solution)/shard_map/shrink/pallas_call | solution.py:242
  43.5 22.9 %scatter_windows.1 = f32[32,32,128]{2,1,0:T(8,128)S(1)} custom-call(f32[8,128]{1,0:T(8,128)S(1)} %get-tuple-element.7.flag, f32[2,64,64,128]{3,2,1,0:T(8,128)S(1)} %bitcast.3), custom_call_target="tpu_custom_call" | custom-call | tf_op jit(solution)/shard_map/scatter_windows/pallas_call | solution.py:757
  66.4 0.8 %copy.12 = f32[32,32,128]{2,1,0:T(8,128)} copy(f32[32,32,128]{2,1,0:T(8,128)S(1)} %scatter_windows.1) | data formatting | bytes 1048576
Async XLA Ops:
  0.0 1.0 %copy-start = (f32[32,32,128]{2,1,0:T(8,128)S(1)}, f32[32,32,128]{2,1,0:T(8,128)}, u32[]{:S(2)}) copy-start(f32[32,32,128]{2,1,0:T(8,128)} %traces.1) | copy-start | bytes 1572868
  1.0 0.7 %copy-start.7 = (s32[32,32]{1,0:T(8,128)S(1)}, s32[32,32]{1,0:T(8,128)}, u32[]{:S(2)}) copy-start(s32[32,32]{1,0:T(8,128)} %flags.1) | copy-start | bytes 12292
  1.8 19.2 %copy-start.1 = (bf16[256,256]{1,0:T(8,128)(2,1)S(1)}, bf16[256,256]{1,0:T(8,128)(2,1)}, u32[]{:S(2)}) copy-start(bf16[256,256]{1,0:T(8,128)(2,1)} %constant.15.clone.time_b) | copy-start | bytes 393220
  1.8 19.2 %copy-start.2 = (bf16[256,256]{1,0:T(8,128)(2,1)S(1)}, bf16[256,256]{1,0:T(8,128)(2,1)}, u32[]{:S(2)}) copy-start(bf16[256,256]{1,0:T(8,128)(2,1)} %constant.14.clone.time_f) | copy-start | bytes 393220
  1.8 19.2 %copy-start.3 = (f32[64,128]{1,0:T(8,128)S(1)}, f32[64,128]{1,0:T(8,128)}, u32[]{:S(2)}) copy-start(f32[64,128]{1,0:T(8,128)} %constant.17.clone.lines) | copy-start | bytes 98308
  1.8 19.2 %copy-start.4 = (f32[64,128]{1,0:T(8,128)S(1)}, f32[64,128]{1,0:T(8,128)}, u32[]{:S(2)}) copy-start(f32[64,128]{1,0:T(8,128)} %constant.16.clone.plane) | copy-start | bytes 98308
  1.8 19.2 %copy-start.5 = (bf16[64,192]{1,0:T(8,128)(2,1)S(1)}, bf16[64,192]{1,0:T(8,128)(2,1)}, u32[]{:S(2)}) copy-start(bf16[64,192]{1,0:T(8,128)(2,1)} %constant.13.clone.space_b) | copy-start | bytes 73732
  1.8 19.2 %copy-start.6 = (bf16[64,192]{1,0:T(8,128)(2,1)S(1)}, bf16[64,192]{1,0:T(8,128)(2,1)}, u32[]{:S(2)}) copy-start(bf16[64,192]{1,0:T(8,128)(2,1)} %constant.12.clone.space_f) | copy-start | bytes 73732
  1.8 19.2 %copy-start.8 = (s32[1,2,2]{2,1,0:T(2,128)S(1)}, s32[1,2,2]{2,1,0:T(2,128)}, u32[]{:S(2)}) copy-start(s32[1,2,2]{2,1,0:T(2,128)} %counts.1) | copy-start | bytes 52
  1.8 19.2 %copy-start.9 = (s32[4]{0:T(128)S(1)}, s32[4]{0:T(128)}, u32[]{:S(2)}) copy-start(s32[4]{0:T(128)} %levels.1) | copy-start | bytes 52
